TPU v7x, 32 devices: a whole 2x2x4 slice. The times are simulated.
32 devices in a mesh: dp: 8 (over z, y), chan: 4 (over x, core).
Axes of the slice: x: 2, y: 2, z: 4, core: 2. Of those that a mesh axis runs over, the one named last changes fastest.
Arguments:
- big_input: float32 [8, 48, 4, 9216], P('dp', 'chan'), may hold values from -6 to 6
- small_input: float32 [8, 48, 4, 4096], P('dp', 'chan'), may hold values from -6 to 6
- spectral_weight: float32 [2, 48, 48, 4, 512], P(None, 'chan'), may hold values from -0.3125 to 0.3125
- point_weight: float32 [48, 48, 4], P('chan'), may hold values from -0.4375 to 0.4375
- point_bias: float32 [48, 4], P('chan'), may hold values from -3 to 3
- big_cotangent: float32 [8, 48, 4, 9216], P('dp', 'chan'), may hold values from -6 to 6
- small_cotangent: float32 [8, 48, 4, 4096], P('dp', 'chan'), may hold values from -6 to 6
- big_live: int32 [8], P('dp'), may hold values from 0 to 1, as said below
- small_live: int32 [8], P('dp'), may hold values from 0 to 1, as said below
Outputs:
- big_out: float32 [8, 48, 4, 9216], P('dp', 'chan')
- small_out: float32 [8, 48, 4, 4096], P('dp', 'chan')
- big_grad: float32 [8, 48, 4, 9216], P('dp', 'chan')
- small_grad: float32 [8, 48, 4, 4096], P('dp', 'chan')
- spectral_grad: float32 [2, 48, 48, 4, 512], P(None, 'chan')
- point_grad: float32 [48, 48, 4], P('chan')
- bias_grad: float32 [48, 4], P('chan')
Inputs may be any that keep to these rules, and one draw needn't show every extreme that they name: `big_live`: each index of dp holds 1 consecutive entries; in every draw one index of dp has all its entries equal to 1. `small_live`: each index of dp holds 1 consecutive entries; in every draw one index of dp has all its entries equal to 1.
All inputs are finite; a program needn't handle non-finite values.
Results may differ from a plain program's by a relative error of at most 0.0003.
Values sent between devices are 32-bit elements; how exact they have to be, the bound alone decides.
A program may use at most 384 MiB of HBM per device.

v0:
```python
import math

import jax
import jax.numpy as jnp
from jax import lax
from jax.sharding import PartitionSpec as P

M = 16
HB = 96
HS = 64


highest = lax.Precision.HIGHEST
blade_index = ((0, 1, 2, 3), (1, 0, 3, 2), (2, 3, 0, 1), (3, 2, 1, 0))
blade_sign = (
    (1.0, 1.0, 1.0, -1.0),
    (1.0, 1.0, 1.0, -1.0),
    (1.0, -1.0, 1.0, 1.0),
    (1.0, -1.0, 1.0, 1.0),
)


def clifford_dense(kernel):
    outer_list = []
    for out_blade in range(4):
        inner_list = [
            blade_sign[out_blade][in_blade] * kernel[:, :, blade_index[out_blade][in_blade]]
            for in_blade in range(4)
        ]
        outer_list.append(jnp.stack(inner_list, axis=2))
    dense_stack = jnp.stack(outer_list, axis=1)
    dense_shape = dense_stack.shape
    return dense_stack.reshape((dense_shape[0] * 4, dense_shape[2] * 4) + dense_shape[4:])


def angle_table(frequencies, positions, length):
    phase_index = frequencies[:, None] * positions[None, :] % length
    angle_value = phase_index.astype(jnp.float32) * (2.0 * math.pi / length)
    return (jnp.cos(angle_value), jnp.sin(angle_value))


def row_frequencies(grid_side):
    low_part = lax.iota(jnp.int32, M)
    return jnp.concatenate([low_part, low_part + (grid_side - M)])


def to_modes(planes, grid_side):
    batch_size, channels, row_count = (planes.shape[0], planes.shape[1], planes.shape[2])
    column_cosine, column_sine = angle_table(
        lax.iota(jnp.int32, M), lax.iota(jnp.int32, grid_side), grid_side
    )
    column_table = jnp.concatenate([column_cosine, -column_sine], axis=0) / grid_side
    along_columns = jnp.einsum("bcrw,jw->bcrj", planes, column_table, precision=highest)
    row_cosine, row_sine = angle_table(
        row_frequencies(grid_side), lax.iota(jnp.int32, row_count), grid_side
    )
    cosine_part = jnp.einsum("kr,bcrj->bckj", row_cosine, along_columns, precision=highest)
    sine_part = jnp.einsum("kr,bcrj->bckj", row_sine, along_columns, precision=highest)
    modes_real = cosine_part[..., :M] + sine_part[..., M:]
    modes_imaginary = cosine_part[..., M:] - sine_part[..., :M]
    return (
        modes_real.reshape(batch_size, channels, 2 * M * M),
        modes_imaginary.reshape(batch_size, channels, 2 * M * M),
    )


def from_modes(modes_real, modes_imaginary, grid_side, row_count):
    batch_size, channels = (modes_real.shape[0], modes_real.shape[1])
    real_grid = modes_real.reshape(batch_size, channels, 2 * M, M)
    imaginary_grid = modes_imaginary.reshape(batch_size, channels, 2 * M, M)
    row_cosine, row_sine = angle_table(
        row_frequencies(grid_side), lax.iota(jnp.int32, row_count), grid_side
    )
    rows_real = jnp.einsum("kr,bckm->bcrm", row_cosine, real_grid, precision=highest) - jnp.einsum(
        "kr,bckm->bcrm", row_sine, imaginary_grid, precision=highest
    )
    rows_imaginary = jnp.einsum(
        "kr,bckm->bcrm", row_cosine, imaginary_grid, precision=highest
    ) + jnp.einsum("kr,bckm->bcrm", row_sine, real_grid, precision=highest)
    column_cosine, column_sine = angle_table(
        lax.iota(jnp.int32, M), lax.iota(jnp.int32, grid_side), grid_side
    )
    column_weight = jnp.where(lax.iota(jnp.int32, M) == 0, 1.0, 2.0) / (2.0 * M)
    column_table = jnp.concatenate(
        [column_cosine * column_weight[:, None], -column_sine * column_weight[:, None]], axis=0
    )
    return jnp.einsum(
        "bcrj,jw->bcrw",
        jnp.concatenate([rows_real, rows_imaginary], axis=-1),
        column_table,
        precision=highest,
    )


def mix_modes(kernel, modes_real, modes_imaginary):
    dense_real = clifford_dense(kernel[0])
    dense_imaginary = clifford_dense(kernel[1])
    mixed_real = jnp.einsum("ojk,bjk->bok", dense_real, modes_real, precision=highest) - jnp.einsum(
        "ojk,bjk->bok", dense_imaginary, modes_imaginary, precision=highest
    )
    mixed_imaginary = jnp.einsum(
        "ojk,bjk->bok", dense_real, modes_imaginary, precision=highest
    ) + jnp.einsum("ojk,bjk->bok", dense_imaginary, modes_real, precision=highest)
    return (mixed_real, mixed_imaginary)


def point_mix(planes, kernel, bias_shard):
    dense_point = clifford_dense(kernel)
    return (
        jnp.einsum("oj,bjp->bop", dense_point, planes, precision=highest)
        + bias_shard.reshape(-1)[None, :, None]
    )


def exact_gelu(values):
    return jax.nn.gelu(values, approximate=False)


def channel_layer(whole, own_field, spectral_weight, point_weight, point_bias, grid_side):
    batch_size = whole.shape[0]
    planes = whole.reshape(batch_size, whole.shape[1] * 4, grid_side, grid_side)
    modes_real, modes_imaginary = to_modes(planes, grid_side)
    mixed_real, mixed_imaginary = mix_modes(spectral_weight, modes_real, modes_imaginary)
    spectral_part = from_modes(mixed_real, mixed_imaginary, grid_side, grid_side).reshape(
        batch_size, -1, grid_side * grid_side
    )
    point_part = point_mix(
        whole.reshape(batch_size, whole.shape[1] * 4, grid_side * grid_side),
        point_weight,
        point_bias,
    )
    flat_own = own_field.reshape(batch_size, -1, grid_side * grid_side)
    return (flat_own + exact_gelu(spectral_part + point_part)).reshape(own_field.shape)


def body(
    big_input,
    small_input,
    spectral_weight,
    point_weight,
    point_bias,
    big_cotangent,
    small_cotangent,
    big_live,
    small_live,
):
    masked_big = big_cotangent * big_live.astype(jnp.float32)[:, None, None, None]
    masked_small = small_cotangent * small_live.astype(jnp.float32)[:, None, None, None]
    whole_big, whole_small = (
        lax.all_gather(big_input, "chan", axis=1, tiled=True),
        lax.all_gather(small_input, "chan", axis=1, tiled=True),
    )
    hidden_big = channel_layer(whole_big, big_input, spectral_weight, point_weight, point_bias, HB)
    hidden_small = channel_layer(
        whole_small, small_input, spectral_weight, point_weight, point_bias, HS
    )
    next_big, next_small = (
        lax.all_gather(hidden_big, "chan", axis=1, tiled=True),
        lax.all_gather(hidden_small, "chan", axis=1, tiled=True),
    )

    def trained(field_big, field_small, own_big, own_small, spec_kernel, point_kernel, bias_vector):
        return (
            channel_layer(field_big, own_big, spec_kernel, point_kernel, bias_vector, HB),
            channel_layer(field_small, own_small, spec_kernel, point_kernel, bias_vector, HS),
        )

    outputs, pullback = jax.vjp(
        trained,
        next_big,
        next_small,
        hidden_big,
        hidden_small,
        spectral_weight,
        point_weight,
        point_bias,
    )
    out_big, out_small = outputs
    back_terms = pullback((masked_big, masked_small))
    spread_big, spread_small = (
        lax.psum_scatter(back_terms[0], "chan", scatter_dimension=1, tiled=True),
        lax.psum_scatter(back_terms[1], "chan", scatter_dimension=1, tiled=True),
    )
    grad_big = spread_big + back_terms[2]
    grad_small = spread_small + back_terms[3]
    grad_spec = back_terms[4]
    grad_point = back_terms[5]
    grad_bias = back_terms[6]
    total_spec, total_point, total_bias = lax.psum((grad_spec, grad_point, grad_bias), "dp")
    dp_count = lax.axis_size("dp")
    sample_total = (big_input.shape[0] + small_input.shape[0]) * dp_count
    pixel_total = (
        big_input.shape[0] * big_input.shape[-1] + small_input.shape[0] * small_input.shape[-1]
    ) * dp_count
    spectral_scale = 1.0 / math.sqrt(sample_total)
    pixel_scale = 1.0 / math.sqrt(pixel_total)
    return (
        out_big,
        out_small,
        grad_big,
        grad_small,
        total_spec * spectral_scale,
        total_point * pixel_scale,
        total_bias * pixel_scale,
    )


def solution(mesh):
    in_specs = (
        P("dp", "chan", None, None),
        P("dp", "chan", None, None),
        P(None, "chan", None, None, None),
        P("chan", None, None),
        P("chan", None),
        P("dp", "chan", None, None),
        P("dp", "chan", None, None),
        P("dp"),
        P("dp"),
    )
    out_specs = (
        P("dp", "chan", None, None),
        P("dp", "chan", None, None),
        P("dp", "chan", None, None),
        P("dp", "chan", None, None),
        P(None, "chan", None, None, None),
        P("chan", None, None),
        P("chan", None),
    )
    return jax.shard_map(body, mesh=mesh, in_specs=in_specs, out_specs=out_specs, check_vma=False)
```

profile of v0, /device:TPU:0, one launch (start us, length us, event | category | flops | bytes accessed | tf_op | source)
XLA Modules:
  0.0 1912.2 jit_solution(3763650568814543064)
XLA Ops:
  71.4 21.7 %reshape.648 = f32[48,192,512]{2,1,0:T(8,128)} reshape(f32[12,4,48,4,512]{4,3,2,1,0:T(4,128)} %copy.173) | data formatting | bytes 37748736 | tf_op jit(solution)/shard_map/reshape | solution.py:33
  93.2 25.2 %copy.273 = f32[48,192,512]{1,0,2:T(8,128)} copy(f32[48,192,512]{2,1,0:T(8,128)} %reshape.648) | data formatting | bytes 37748736 | tf_op jit(solution)/shard_map/reshape | solution.py:33
  146.1 21.7 %reshape.646 = f32[48,192,512]{2,1,0:T(8,128)} reshape(f32[12,4,48,4,512]{4,3,2,1,0:T(4,128)} %copy.171) | data formatting | bytes 37748736 | tf_op jit(solution)/shard_map/reshape | solution.py:33
  167.8 25.2 %copy.270 = f32[48,192,512]{1,0,2:T(8,128)} copy(f32[48,192,512]{2,1,0:T(8,128)} %reshape.646) | data formatting | bytes 37748736 | tf_op jit(solution)/shard_map/reshape | solution.py:33
  223.3 25.2 %fusion.155 = f32[512,1,48]{2,1,0:T(1,128)S(1)} fusion(f32[48,192,512]{1,0,2:T(8,128)} %copy.273, f32[192,512,1]{0,1,2:T(8,128)S(1)} %bitcast.791), kind=kOutput, calls=%fused_computation.288 | convolution fusion | flops 56623104 | bytes 19365888 | tf_op jit(solution)/shard_map/ojk,bjk->bok/dot_general | solution.py:103
  248.5 20.8 %fusion.153 = f32[512,1,48]{2,1,0:T(1,128)S(1)} fusion(f32[48,192,512]{1,0,2:T(8,128)S(1)} %bitcast.745, f32[192,512,1]{0,1,2:T(8,128)S(1)} %bitcast.793), kind=kOutput, calls=%fused_computation.286 | convolution fusion | flops 56623104 | bytes 19365888 | tf_op jit(solution)/shard_map/ojk,bjk->bok/dot_general | solution.py:98
  269.4 23.9 %fusion.151 = f32[512,1,48]{2,1,0:T(1,128)S(1)} fusion(f32[48,192,512]{1,0,2:T(8,128)} %copy.270, f32[192,512,1]{0,1,2:T(8,128)S(1)} %bitcast.794), kind=kOutput, calls=%fused_computation.284 | convolution fusion | flops 56623104 | bytes 19365888 | tf_op jit(solution)/shard_map/ojk,bjk->bok/dot_general | solution.py:101
  293.2 24.1 %fusion.157 = f32[512,1,48]{2,1,0:T(1,128)S(1)} fusion(f32[48,192,512]{1,0,2:T(8,128)} %copy.270, f32[192,512,1]{0,1,2:T(8,128)S(1)} %bitcast.792), kind=kOutput, calls=%fused_computation.290 | convolution fusion | flops 56623104 | bytes 19365888 | tf_op jit(solution)/shard_map/ojk,bjk->bok/dot_general | solution.py:98
  347.5 21.1 %all-gather.11.cloned.1.call-done = f32[1,48,4,4096]{3,2,0,1:T(4,128)} async-done(((f32[1,12,4,4096]{3,2,0,1:T(4,128)}), f32[1,48,4,4096]{3,2,0,1:T(4,128)}) %all-gather.11.cloned.1.call-update) | async-done | bytes 3145744 | tf_op jit(solution)/shard_map/all_gather | solution.py:159
  398.2 23.6 %fusion.147 = f32[512,1,48]{2,1,0:T(1,128)S(1)} fusion(f32[48,192,512]{1,0,2:T(8,128)} %copy.273, f32[192,512,1]{0,1,2:T(8,128)S(1)} %bitcast.788), kind=kOutput, calls=%fused_computation.280 | convolution fusion | flops 56623104 | bytes 19365888 | tf_op jit(solution)/shard_map/jvp(ojk,bjk->bok)/dot_general | solution.py:103
  421.9 24.0 %fusion.149 = f32[512,1,48]{2,1,0:T(1,128)S(1)} fusion(f32[48,192,512]{1,0,2:T(8,128)} %copy.270, f32[192,512,1]{0,1,2:T(8,128)S(1)} %bitcast.789), kind=kOutput, calls=%fused_computation.282 | convolution fusion | flops 56623104 | bytes 19365888 | tf_op jit(solution)/shard_map/jvp(ojk,bjk->bok)/dot_general | solution.py:98
  446.3 23.8 %fusion.143 = f32[512,1,48]{2,1,0:T(1,128)S(1)} fusion(f32[48,192,512]{1,0,2:T(8,128)} %copy.270, f32[192,512,1]{0,1,2:T(8,128)S(1)} %bitcast.785), kind=kOutput, calls=%fused_computation.276 | convolution fusion | flops 56623104 | bytes 19365888 | tf_op jit(solution)/shard_map/jvp(ojk,bjk->bok)/dot_general | solution.py:101
  470.2 21.5 %fusion.145 = f32[512,1,48]{2,1,0:T(1,128)S(1)} fusion(f32[48,192,512]{1,0,2:T(8,128)S(1)} %bitcast.747, f32[192,512,1]{0,1,2:T(8,128)S(1)} %bitcast.786), kind=kOutput, calls=%fused_computation.278 | convolution fusion | flops 56623104 | bytes 19365888 | tf_op jit(solution)/shard_map/jvp(ojk,bjk->bok)/dot_general | solution.py:98
  635.9 21.3 %reshape.720 = f32[12,4,48,4,512]{4,3,2,1,0:T(4,128)} reshape(f32[48,192,512]{2,1,0:T(8,128)} %get-tuple-element.144) | data formatting | bytes 37748736 | tf_op jit(solution)/shard_map/transpose(jvp())/reshape | solution.py:33
  657.2 21.3 %reshape.721 = f32[12,4,48,4,512]{4,3,2,1,0:T(4,128)} reshape(f32[48,192,512]{2,1,0:T(8,128)} %get-tuple-element.145) | data formatting | bytes 37748736 | tf_op jit(solution)/shard_map/transpose(jvp())/reshape | solution.py:33
  717.9 22.2 %convolution_bitcast_fusion.6 = f32[192,96,32]{1,2,0:T(8,128)S(1)} fusion(f32[192,96,96]{2,1,0:T(8,128)} %reshape.644, f32[16,96]{1,0:T(8,128)S(1)} %copy-done.66, f32[16,96]{1,0:T(8,128)S(1)} %copy-done.68), kind=kOutput, calls=%fused_computation.91 | convolution fusion | flops 679483392 | bytes 9449472 | tf_op jit(solution)/shard_map/bcrw,jw->bcrj/dot_general | solution.py:53
  754.8 25.2 %fusion.169 = f32[512,1,48]{2,1,0:T(1,128)S(1)} fusion(f32[48,192,512]{1,0,2:T(8,128)} %copy.273, f32[192,512,1]{0,1,2:T(8,128)S(1)} %bitcast.795), kind=kOutput, calls=%fused_computation.302 | convolution fusion | flops 56623104 | bytes 19365888 | tf_op jit(solution)/shard_map/ojk,bjk->bok/dot_general | solution.py:98
  780.1 23.8 %fusion.167 = f32[512,1,48]{2,1,0:T(1,128)S(1)} fusion(f32[48,192,512]{1,0,2:T(8,128)} %copy.270, f32[192,512,1]{0,1,2:T(8,128)S(1)} %bitcast.796), kind=kOutput, calls=%fused_computation.300 | convolution fusion | flops 56623104 | bytes 19365888 | tf_op jit(solution)/shard_map/ojk,bjk->bok/dot_general | solution.py:101
  804.3 21.0 %fusion.171 = f32[512,1,48]{2,1,0:T(1,128)S(1)} fusion(f32[48,192,512]{1,0,2:T(8,128)S(1)} %bitcast.751, f32[192,512,1]{0,1,2:T(8,128)S(1)} %bitcast.797), kind=kOutput, calls=%fused_computation.304 | convolution fusion | flops 56623104 | bytes 19365888 | tf_op jit(solution)/shard_map/ojk,bjk->bok/dot_general | solution.py:103
  825.3 24.1 %fusion.173 = f32[512,1,48]{2,1,0:T(1,128)S(1)} fusion(f32[48,192,512]{1,0,2:T(8,128)} %copy.270, f32[192,512,1]{0,1,2:T(8,128)S(1)} %bitcast.798), kind=kOutput, calls=%fused_computation.306 | convolution fusion | flops 56623104 | bytes 19365888 | tf_op jit(solution)/shard_map/ojk,bjk->bok/dot_general | solution.py:98
  926.7 19.8 %add_bitcast_fusion.6 = f32[1,12,48,4,512]{4,3,2,1,0:T(4,128)} fusion(f32[12,48,1,512]{3,2,1,0:T(1,128)} %get-tuple-element.84, f32[12,48,1,512]{3,2,1,0:T(1,128)} %get-tuple-element.85, f32[12,48,1,512]{3,2,1,0:T(1,128)S(1)} %copy-done.46, f32[12,48,1,512]{3,2,1,0:T(1,128)S(1)} %get-tuple-element.80, f32[12,48,1,512]{3,2,1,0:T(1,128)S(1)} %get-tuple-element.81, ...), kind=kLoop, calls=%fused_computation.51 | loop fusion | flops 18874368 | bytes 27131908 | tf_op jit(solution)/shard_map/transpose(jvp())/broadcast_in_dim | solution.py:96
  976.1 22.1 %fusion.272 = f32[192,96,32]{1,2,0:T(8,128)S(1)} fusion(f32[192,96,96]{2,1,0:T(8,128)} %reshape.656, f32[16,96]{1,0:T(8,128)S(1)} %copy-done.66, f32[16,96]{1,0:T(8,128)S(1)} %copy-done.68), kind=kOutput, calls=%fused_computation.413 | convolution fusion | flops 679483392 | bytes 9449472 | tf_op jit(solution)/shard_map/jvp(bcrw,jw->bcrj)/dot_general | solution.py:53
  1012.9 23.8 %fusion.163 = f32[512,1,48]{2,1,0:T(1,128)S(1)} fusion(f32[48,192,512]{1,0,2:T(8,128)} %copy.273, f32[192,512,1]{0,1,2:T(8,128)S(1)} %bitcast.779), kind=kOutput, calls=%fused_computation.296 | convolution fusion | flops 56623104 | bytes 19365888 | tf_op jit(solution)/shard_map/jvp(ojk,bjk->bok)/dot_general | solution.py:103
  1036.7 23.8 %fusion.165 = f32[512,1,48]{2,1,0:T(1,128)S(1)} fusion(f32[48,192,512]{1,0,2:T(8,128)} %copy.270, f32[192,512,1]{0,1,2:T(8,128)S(1)} %bitcast.780), kind=kOutput, calls=%fused_computation.298 | convolution fusion | flops 56623104 | bytes 19365888 | tf_op jit(solution)/shard_map/jvp(ojk,bjk->bok)/dot_general | solution.py:98
  1060.9 24.1 %fusion.159 = f32[512,1,48]{2,1,0:T(1,128)S(1)} fusion(f32[48,192,512]{1,0,2:T(8,128)} %copy.270, f32[192,512,1]{0,1,2:T(8,128)S(1)} %bitcast.782), kind=kOutput, calls=%fused_computation.292 | convolution fusion | flops 56623104 | bytes 19365888 | tf_op jit(solution)/shard_map/jvp(ojk,bjk->bok)/dot_general | solution.py:101
  1085.1 21.3 %fusion.161 = f32[512,1,48]{2,1,0:T(1,128)S(1)} fusion(f32[48,192,512]{1,0,2:T(8,128)S(1)} %bitcast.753, f32[192,512,1]{0,1,2:T(8,128)S(1)} %bitcast.783), kind=kOutput, calls=%fused_computation.294 | convolution fusion | flops 56623104 | bytes 19365888 | tf_op jit(solution)/shard_map/jvp(ojk,bjk->bok)/dot_general | solution.py:98
  1296.9 21.3 %reshape.722 = f32[12,4,48,4,512]{4,3,2,1,0:T(4,128)} reshape(f32[48,192,512]{2,1,0:T(8,128)} %get-tuple-element.146) | data formatting | bytes 37748736 | tf_op jit(solution)/shard_map/transpose(jvp())/reshape | solution.py:33
  1318.2 21.6 %reshape.723 = f32[12,4,48,4,512]{4,3,2,1,0:T(4,128)} reshape(f32[48,192,512]{2,1,0:T(8,128)} %get-tuple-element.147) | data formatting | bytes 37748736 | tf_op jit(solution)/shard_map/transpose(jvp())/reshape | solution.py:33
  1418.0 19.3 %add_bitcast_fusion.4 = f32[1,12,48,4,512]{4,3,2,1,0:T(4,128)S(1)} fusion(f32[12,48,1,512]{3,2,1,0:T(1,128)} %get-tuple-element.114, f32[12,48,1,512]{3,2,1,0:T(1,128)} %get-tuple-element.115, f32[12,48,1,512]{3,2,1,0:T(1,128)} %get-tuple-element.113, f32[12,48,1,512]{3,2,1,0:T(1,128)S(1)} %copy-done.25, f32[12,48,1,512]{3,2,1,0:T(1,128)S(1)} %copy-done.26, ...), kind=kLoop, calls=%fused_computation.49 | loop fusion | flops 18874368 | bytes 27131908 | tf_op jit(solution)/shard_map/transpose(jvp())/broadcast_in_dim | solution.py:96
  1502.8 37.3 %all-reduce.104 = (f32[12,48,4]{1,0,2:T(8,128)S(1)}, f32[12,4]{1,0:T(8,128)S(1)}) all-reduce(f32[12,48,4]{1,0,2:T(8,128)S(1)} %select_add_fusion, f32[12,4]{1,0:T(8,128)S(1)} %add_any.583), channel_id=1, replica_groups=mesh['dp'=8,'chan'=4] {'dp'}, use_global_device_ids=true, to_apply=%region_3.4 | all-reduce | flops 2352 | bytes 18816 | tf_op jit(solution)/shard_map/psum | solution.py:189
  1541.4 50.0 %all-reduce.111.cloned.1.call-done = (f32[1,48,4,9216]{3,2,1,0:T(4,128)}, f32[1,48,4,4096]{3,2,1,0:T(4,128)}) async-done(((f32[1,48,4,9216]{3,2,1,0:T(4,128)}, f32[1,48,4,4096]{3,2,1,0:T(4,128)}), (f32[1,48,4,9216]{3,2,1,0:T(4,128)}, f32[1,48,4,4096]{3,2,1,0:T(4,128)})) %all-reduce.111.cloned.1.call-update) | async-done | bytes 10223632
  1597.0 297.0 %all-reduce.109.cloned.1.call-done = f32[2,12,48,4,512]{4,3,2,1,0:T(4,128)} async-done(((f32[2,12,48,4,512]{4,3,2,1,0:T(4,128)}), f32[2,12,48,4,512]{4,3,2,1,0:T(4,128)}) %all-reduce.109.cloned.1.call-update) | async-done | bytes 9437200 | tf_op jit(solution)/shard_map/psum | solution.py:189
  (589 shorter events, 850.2 us)
Async XLA Ops:
  7.2 186.7 %all-gather.9.cloned.1.call-start = ((), (), s32[]{:S(2)}) async-start(), calls=%async_computation.2 | async-start | bytes 3932160 | tf_op jit(solution)/shard_map/all_gather | solution.py:151
  7.9 360.7 %all-gather.11.cloned.1.call-start = ((), (), s32[]{:S(2)}) async-start(), calls=%async_computation.3 | async-start | bytes 3932160 | tf_op jit(solution)/shard_map/all_gather | solution.py:159
  93.2 25.2 %copy-start.7 = (f32[12,48,2,512]{3,2,1,0:T(2,128)S(1)}, f32[12,48,2,512]{3,2,1,0:T(2,128)}, u32[]{:S(2)}) copy-start(f32[12,48,2,512]{3,2,1,0:T(2,128)} %slice.127) | copy-start | bytes 7077892
  93.2 25.2 %copy-start.19 = (f32[12,48,1,512]{3,2,1,0:T(1,128)S(1)}, f32[12,48,1,512]{3,2,1,0:T(1,128)}, u32[]{:S(2)}) copy-start(f32[12,48,1,512]{3,2,1,0:T(1,128)} %get-tuple-element.220) | copy-start | bytes 3538948
  193.8 127.2 %copy-start.72 = (f32[16,64]{1,0:T(8,128)}, f32[16,64]{1,0:T(8,128)S(1)}, u32[]{:S(2)}) copy-start(f32[16,64]{1,0:T(8,128)S(1)} %get-tuple-element.209) | copy-start | bytes 12292
  222.4 26.1 %slice-start = ((s8[25165824]{0:T(1024)(128)(4,1)}), s8[4194304]{0:T(1024)(128)(4,1)S(1)}, s32[]{:S(2)}) async-start(s8[25165824]{0:T(1024)(128)(4,1)} %bitcast.744), calls=%async_computation.6 | async-start | bytes 8388608
  223.2 25.3 %slice-start.1 = ((s8[25165824]{0:T(1024)(128)(4,1)}), s8[4194304]{0:T(1024)(128)(4,1)S(1)}, s32[]{:S(2)}) async-start(s8[25165824]{0:T(1024)(128)(4,1)} %bitcast.744), calls=%async_computation.7 | async-start | bytes 8388608
  223.2 25.3 %slice-start.2 = ((s8[25165824]{0:T(1024)(128)(4,1)}), s8[4194304]{0:T(1024)(128)(4,1)S(1)}, s32[]{:S(2)}) async-start(s8[25165824]{0:T(1024)(128)(4,1)} %bitcast.744), calls=%async_computation.8 | async-start | bytes 8388608
  223.2 25.3 %slice-start.3 = ((s8[25165824]{0:T(1024)(128)(4,1)}), s8[4194304]{0:T(1024)(128)(4,1)S(1)}, s32[]{:S(2)}) async-start(s8[25165824]{0:T(1024)(128)(4,1)} %bitcast.744), calls=%async_computation.9 | async-start | bytes 8388608
  223.2 25.3 %slice-start.4 = ((s8[25165824]{0:T(1024)(128)(4,1)}), s8[4194304]{0:T(1024)(128)(4,1)S(1)}, s32[]{:S(2)}) async-start(s8[25165824]{0:T(1024)(128)(4,1)} %bitcast.744), calls=%async_computation.10 | async-start | bytes 8388608
  223.2 25.3 %slice-start.5 = ((s8[25165824]{0:T(1024)(128)(4,1)}), s8[4194304]{0:T(1024)(128)(4,1)S(1)}, s32[]{:S(2)}) async-start(s8[25165824]{0:T(1024)(128)(4,1)} %bitcast.744), calls=%async_computation.11 | async-start | bytes 8388608
  337.4 370.0 %all-gather.5.cloned.1.call-start = ((), (), s32[]{:S(2)}) async-start(), calls=%async_computation | async-start | bytes 8847360 | tf_op jit(solution)/shard_map/all_gather | solution.py:150
  338.2 627.5 %all-gather.7.cloned.1.call-start = ((), (), s32[]{:S(2)}) async-start(), calls=%async_computation.1 | async-start | bytes 8847360 | tf_op jit(solution)/shard_map/all_gather | solution.py:158
  347.5 27.5 %copy-start.75 = (f32[16,64]{1,0:T(8,128)S(1)}, f32[16,64]{1,0:T(8,128)}, u32[]{:S(2)}) copy-start(f32[16,64]{1,0:T(8,128)} %copy-done.74) | copy-start | bytes 12292
  347.5 27.5 %copy-start.78 = (f32[16,64]{1,0:T(8,128)S(1)}, f32[16,64]{1,0:T(8,128)}, u32[]{:S(2)}) copy-start(f32[16,64]{1,0:T(8,128)} %copy-done.77) | copy-start | bytes 12292
  421.9 48.2 %slice-start.6 = ((s8[25165824]{0:T(1024)(128)(4,1)}), s8[4194304]{0:T(1024)(128)(4,1)S(1)}, s32[]{:S(2)}) async-start(s8[25165824]{0:T(1024)(128)(4,1)} %bitcast.746), calls=%async_computation.12 | async-start | bytes 8388608
  421.9 48.2 %slice-start.7 = ((s8[25165824]{0:T(1024)(128)(4,1)}), s8[4194304]{0:T(1024)(128)(4,1)S(1)}, s32[]{:S(2)}) async-start(s8[25165824]{0:T(1024)(128)(4,1)} %bitcast.746), calls=%async_computation.13 | async-start | bytes 8388608
  421.9 48.2 %slice-start.8 = ((s8[25165824]{0:T(1024)(128)(4,1)}), s8[4194304]{0:T(1024)(128)(4,1)S(1)}, s32[]{:S(2)}) async-start(s8[25165824]{0:T(1024)(128)(4,1)} %bitcast.746), calls=%async_computation.14 | async-start | bytes 8388608
  514.8 98.6 %copy-start.14 = (f32[1,48,4096]{2,1,0:T(8,128)}, f32[1,48,4096]{2,1,0:T(8,128)S(1)}, u32[]{:S(2)}) copy-start(f32[1,48,4096]{2,1,0:T(8,128)S(1)} %get-tuple-element.36) | copy-start | bytes 2359300
  754.8 49.4 %slice-start.18 = ((s8[25165824]{0:T(1024)(128)(4,1)}), s8[4194304]{0:T(1024)(128)(4,1)S(1)}, s32[]{:S(2)}) async-start(s8[25165824]{0:T(1024)(128)(4,1)} %bitcast.750), calls=%async_computation.24 | async-start | bytes 8388608
  754.8 49.4 %slice-start.19 = ((s8[25165824]{0:T(1024)(128)(4,1)}), s8[4194304]{0:T(1024)(128)(4,1)S(1)}, s32[]{:S(2)}) async-start(s8[25165824]{0:T(1024)(128)(4,1)} %bitcast.750), calls=%async_computation.25 | async-start | bytes 8388608
  754.8 49.4 %slice-start.20 = ((s8[25165824]{0:T(1024)(128)(4,1)}), s8[4194304]{0:T(1024)(128)(4,1)S(1)}, s32[]{:S(2)}) async-start(s8[25165824]{0:T(1024)(128)(4,1)} %bitcast.750), calls=%async_computation.26 | async-start | bytes 8388608
  880.2 711.2 %all-reduce.111.cloned.1.call-start = ((), (), s32[]{:S(2)}) async-start(), calls=%async_computation.5 | async-start | bytes 20447232
  1036.7 48.3 %slice-start.24 = ((s8[25165824]{0:T(1024)(128)(4,1)}), s8[4194304]{0:T(1024)(128)(4,1)S(1)}, s32[]{:S(2)}) async-start(s8[25165824]{0:T(1024)(128)(4,1)} %bitcast.752), calls=%async_computation.30 | async-start | bytes 8388608
  1036.7 48.3 %slice-start.25 = ((s8[25165824]{0:T(1024)(128)(4,1)}), s8[4194304]{0:T(1024)(128)(4,1)S(1)}, s32[]{:S(2)}) async-start(s8[25165824]{0:T(1024)(128)(4,1)} %bitcast.752), calls=%async_computation.31 | async-start | bytes 8388608
  1036.7 48.3 %slice-start.26 = ((s8[25165824]{0:T(1024)(128)(4,1)}), s8[4194304]{0:T(1024)(128)(4,1)S(1)}, s32[]{:S(2)}) async-start(s8[25165824]{0:T(1024)(128)(4,1)} %bitcast.752), calls=%async_computation.32 | async-start | bytes 8388608
  1140.2 45.4 %copy-start.4 = (f32[1,48,9216]{2,1,0:T(8,128)}, f32[1,48,9216]{2,1,0:T(8,128)S(1)}, u32[]{:S(2)}) copy-start(f32[1,48,9216]{2,1,0:T(8,128)S(1)} %get-tuple-element.33) | copy-start | bytes 5308420
  1142.5 30.0 %slice-start.30 = ((s8[25165824]{0:T(1024)(128)(4,1)}), s8[4194304]{0:T(1024)(128)(4,1)S(1)}, s32[]{:S(2)}) async-start(s8[25165824]{0:T(1024)(128)(4,1)} %bitcast.754), calls=%async_computation.36 | async-start | bytes 8388608
  1408.5 485.5 %all-reduce.109.cloned.1.call-start = ((), (), s32[]{:S(2)}) async-start(), calls=%async_computation.4 | async-start | bytes 18874368 | tf_op jit(solution)/shard_map/psum | solution.py:189
  1418.0 37.3 %slice-start.58 = ((s8[4718592]{0:T(1024)(128)(4,1)}), s8[4194304]{0:T(1024)(128)(4,1)S(1)}, s32[]{:S(2)}) async-start(s8[4718592]{0:T(1024)(128)(4,1)} %bitcast.775), calls=%async_computation.64 | async-start | bytes 8388608
  1418.0 37.3 %slice-start.60 = ((s8[4718592]{0:T(1024)(128)(4,1)}), s8[4194304]{0:T(1024)(128)(4,1)S(1)}, s32[]{:S(2)}) async-start(s8[4718592]{0:T(1024)(128)(4,1)} %bitcast.777), calls=%async_computation.66 | async-start | bytes 8388608
  1501.5 92.3 %copy-start.13 = (f32[1,12,4,9216]{3,2,1,0:T(4,128)S(1)}, f32[1,12,4,9216]{3,2,1,0:T(4,128)}, u32[]{:S(2)}) copy-start(f32[1,12,4,9216]{3,2,1,0:T(4,128)} %param.14) | copy-start | bytes 5308420
  (140 other events, 1721.6 us)
Sparse Core Ops, SparseCore 0:
  9.6 31.2 all-gather.8
  337.5 31.0 all-gather.10
  370.2 50.8 all-gather.4
  880.3 50.6 all-gather.6
  1408.6 182.7 all-reduce.110
  1595.6 298.3 all-reduce.108
where the time goes:
time: 1920 us; the launch traced here: 1910 us
  matrix products  787 us (41%)
  local copies, waits for them, and re-layouts  384 us (20%)
  waiting for transfers between devices  370 us (19%)
  other arithmetic  315 us (16%)
  blocking collectives  37.3 us (2%)
  between operations  19.6 us (1%)
    psum x1, waiting for transfers between devices, body(): lax.psum((grad_spec, grad_point, grad_bias), 'dp')  297 us
    reshape x9, local copies, waits for them, and re-layouts, clifford_dense(): dense_stack.reshape((dense_shape[0] * 4, dense_shape[2] * 4) + dense_shap...  181 us
    dot_general x6, matrix products, mix_modes(): jnp.einsum('ojk,bjk->bok', dense_real, modes_real, precision=highest)  127 us
    dot_general x6, matrix products, mix_modes(): jnp.einsum('ojk,bjk->bok', dense_real, modes_imaginary, precision=highest)  125 us
    dot_general x6, matrix products, mix_modes(): jnp.einsum('ojk,bjk->bok', dense_imaginary, modes_real, precision=highest)  124 us
    dot_general x6, matrix products, mix_modes(): jnp.einsum('ojk,bjk->bok', dense_imaginary, modes_imaginary, precision=hi...  120 us
    dot_general x6, matrix products, to_modes(): jnp.einsum('bcrw,jw->bcrj', planes, column_table, precision=highest)  103 us
    dot_general x8, matrix products, point_mix(): jnp.einsum('oj,bjp->bop', dense_point, planes, precision=highest)  76.6 us
  transfers between devices with their start and end apart: 6, of which 3 were waited for; matrix products, arithmetic and copies ran while one was open for 37% of the time, Pallas kernels for 0%

commit v1 on v0

v1 whole, which is shorter than its diff:
```python
import functools
import math

import jax
import jax.numpy as jnp
import ml_dtypes
import numpy as np
from jax import lax
from jax.experimental import pallas as pl
from jax.experimental.pallas import tpu as pltpu
from jax.sharding import PartitionSpec as P

M = 16
MODES = 2 * M * M
HB = 96
HS = 64
CB = HB // 8
CS = HS // 8
LB = 8 * HB
LS = 8 * HS
NB = HB * HB // 4
NS = HS * HS // 4
NQ = NB + NS
TILES = 4
NEAR = 5
PG = 384
VMEM_LIMIT = 62 * 1024 * 1024

def mode_numbers():
    mode = np.arange(MODES)
    row = mode // M
    return np.where(row < M, row, row - 2 * M), mode % M


def pair_of(table):
    high = table.astype(ml_dtypes.bfloat16)
    return high, (table - high.astype(np.float64)).astype(ml_dtypes.bfloat16)


def column_table(side):
    cell, out = np.arange(8 * side), np.arange(8 * M)
    angle = np.outer(cell % side, out % M) % side * (2.0 * np.pi / side)
    same = np.equal.outer(cell // side, out // M)
    return np.concatenate([np.cos(angle) * same, -np.sin(angle) * same], axis=1)


def row_table(side):
    k, l = mode_numbers()
    row = np.arange(8 * M)
    angle = np.outer(row // M, k) % side * (2.0 * np.pi / side)
    same = np.equal.outer(row % M, l)
    cos, sin = np.cos(angle) * same, np.sin(angle) * same
    real = np.concatenate([cos, sin], axis=0).reshape(2 * 8 * M, TILES, 128)
    imag = np.concatenate([-sin, cos], axis=0).reshape(2 * 8 * M, TILES, 128)
    return np.stack([real, imag], axis=2).reshape(2 * 8 * M, 2 * MODES)


def chunk_phase(side, kind):
    k, l = mode_numbers()
    chunk = np.arange(side // 8)
    angle = (np.outer(8 * chunk, k) % side) * (2.0 * np.pi / side)
    scale = 1.0 / side if kind == "in" else np.where(l == 0, 1.0, 2.0) / (2.0 * M)
    return np.stack([np.cos(angle) * scale, np.sin(angle) * scale], axis=1).astype(np.float32)


def interleave(channels):
    table = np.zeros((4, 128, 256), ml_dtypes.bfloat16)
    for blade in range(4):
        for channel in range(channels):
            table[blade, channel, 4 * channel + blade] = 1
    return table


def split(value):
    high = value.astype(jnp.bfloat16)
    return high, (value - high.astype(jnp.float32)).astype(jnp.bfloat16)


def dot3(ah, al, bh, bl, dims=(((1,), (0,)), ((), ()))):
    dot = functools.partial(lax.dot_general, dimension_numbers=dims, preferred_element_type=jnp.float32)
    return dot(ah, bh) + (dot(ah, bl) + dot(al, bh))


NT = (((1,), (1,)), ((), ()))


def first_stage(h, l, th, tl, yh, yl, used):
    yh[used, :], yl[used, :] = split(dot3(h, l, th[...], tl[...]))


def forward_tile(yh, yl, vh, vl, phase, chunk0, count, rows, t):
    cols = pl.ds(pl.multiple_of(256 * t, 256), 256)
    used = slice(0, count * rows)
    local = dot3(yh[used, :], yl[used, :], vh[:, cols], vl[:, cols])
    lanes = pl.ds(pl.multiple_of(128 * t, 128), 128)
    re = im = None
    for j in range(count):
        lr = local[rows * j : rows * (j + 1), :128]
        li = local[rows * j : rows * (j + 1), 128:]
        cos = phase[chunk0 + j, 0:1, lanes]
        sin = phase[chunk0 + j, 1:2, lanes]
        pr = lr * cos + li * sin
        pi = li * cos - lr * sin
        re, im = (pr, pi) if re is None else (re + pr, im + pi)
    return re, im


def turn_modes(z_ref, zh, zl, phase, chunk, s, rows, row0):
    def tile(t, _):
        lanes = pl.ds(pl.multiple_of(128 * t, 128), 128)
        zr = z_ref[t, :, 256 * s : 256 * s + 128]
        zi = z_ref[t, :, 256 * s + 128 : 256 * s + 256]
        cos = phase[chunk, 0:1, lanes]
        sin = phase[chunk, 1:2, lanes]
        for part, value in enumerate((zr * cos - zi * sin, zr * sin + zi * cos)):
            high, low = split(value)
            where = pl.ds(pl.multiple_of(256 * t + 128 * part, 128), 128)
            zh[row0 : row0 + rows, where] = high
            zl[row0 : row0 + rows, where] = low
        return 0

    lax.fori_loop(0, TILES, tile, 0)


class Lanes:
    def __init__(self):
        sub = lax.broadcasted_iota(jnp.int32, (8, 128), 0)
        self.sub, self.s4 = sub, sub % 4
        self.even = sub % 2 == 0
        self.low = sub % 4 < 2
        self.half = sub < 4
        self.sign = jnp.where(self.even, 1.0, -1.0).astype(jnp.float32)
        self.sign_own = jnp.where(self.s4 == 1, -1.0, 1.0).astype(jnp.float32)
        self.sign_other = jnp.where(self.s4 == 2, -1.0, 1.0).astype(jnp.float32)
        self.by = {k: jnp.bitwise_xor(sub, k) for k in (1, 2, 3, 4)}

    def swap(self, x, k):
        return jnp.take_along_axis(x, self.by[k], axis=0)

    def to_matrix(self, x):
        return x * self.sign + self.swap(x, 1)

    def to_entries(self, x):
        return x * self.sign_own + self.swap(x, 1) * self.sign_other

    def columns(self, m):
        m3 = self.swap(m, 3)
        return jnp.where(self.even, m, m3), jnp.where(self.even, m3, m)


def mix_tile(wm, t, load, z_ref, me, xe, ln):
    groups = xe.shape[3] // 8
    outs = wm.shape[2]

    def expand(g, _):
        rows = pl.ds(pl.multiple_of(8 * g, 8), 8)
        for s in range(2):
            parts = []
            for ri in range(2):
                lanes = slice(256 * s + 128 * ri, 256 * s + 128 * ri + 128)
                parts.append(ln.columns(load(rows, lanes)))
            for c in range(2):
                xe[s, c, 0, rows, :] = parts[0][c]
                xe[s, c, 1, rows, :] = parts[1][c]
                xe[s, c, 2, rows, :] = parts[0][c] + parts[1][c]
        return 0

    lax.fori_loop(0, groups, expand, 0)

    def pair(p, _):
        acc = {}
        for g in range(groups):
            rows = slice(8 * g, 8 * g + 8)
            w = []
            for a in range(2):
                wr, wi = wm[t, 0, 2 * p + a, rows, :], wm[t, 1, 2 * p + a, rows, :]
                w.append((wr, wi, wr + wi))
            for s in range(2):
                for c in range(2):
                    for q in range(3):
                        x = xe[s, c, q, rows, :]
                        for a in range(2):
                            key = (a, s, c, q)
                            acc[key] = w[a][q] * x + acc[key] if key in acc else w[a][q] * x
        rows = pl.ds(pl.multiple_of(4 * outs * me + 8 * p, 8), 8)
        for s in range(2):
            for ri in range(2):
                out = []
                for a in range(2):
                    red = []
                    for c in range(2):
                        t1, t2, t3 = (acc[a, s, c, q] for q in range(3))
                        value = t1 - t2 if ri == 0 else t3 - t1 - t2
                        value = value + ln.swap(value, 4)
                        red.append(value + ln.swap(value, 2))
                    first = jnp.where(ln.low, red[0], red[1])
                    first = jnp.where(ln.even, first, ln.swap(first, 1))
                    second = jnp.where(ln.low, red[1], red[0])
                    second = jnp.where(ln.even, ln.swap(second, 1), second)
                    out.append(0.5 * (first + ln.sign * second))
                z_ref[t, rows, 256 * s + 128 * ri : 256 * s + 128 * ri + 128] = jnp.where(ln.half, out[0], out[1])
        return 0

    lax.fori_loop(0, outs // 2, pair, 0)


def both_outputs(d, ln):
    turned = ln.swap(d, 4)
    return jnp.where(ln.half, d, turned), jnp.where(ln.half, turned, d)


def unmix_tile(wm, t, d_ref, x_ref, de, ln):
    groups = x_ref.shape[1] // 8
    outs = wm.shape[2]

    def expand(p, _):
        rows = pl.ds(pl.multiple_of(8 * p, 8), 8)
        for s in range(2):
            vals = []
            for ri in range(2):
                m = ln.to_matrix(d_ref[t, rows, 256 * s + 128 * ri : 256 * s + 128 * ri + 128])
                vals.append(both_outputs(m, ln))
            for a in range(2):
                pats = []
                for ri in range(2):
                    m = vals[ri][a]
                    m2 = ln.swap(m, 2)
                    outer = (ln.s4 == 0) | (ln.s4 == 3)
                    pats.append((jnp.where(outer, m, m2), jnp.where(outer, m2, m)))
                for c in range(2):
                    here = pl.ds(pl.multiple_of(16 * p + 8 * a, 8), 8)
                    de[s, c, 0, here, :] = pats[0][c]
                    de[s, c, 1, here, :] = pats[1][c]
                    de[s, c, 2, here, :] = pats[0][c] + pats[1][c]
        return 0

    lax.fori_loop(0, outs // 2, expand, 0)

    def pair(p, _):
        acc = {}
        for o in range(outs):
            w = []
            for a in range(2):
                where = pl.ds(pl.multiple_of(16 * p + 8 * a, 8), 8)
                wr, wi = wm[t, 0, o, where, :], wm[t, 1, o, where, :]
                w.append((wr, wi, wr - wi))
            for s in range(2):
                for c in range(2):
                    for q in range(3):
                        d = de[s, c, q, 8 * o : 8 * o + 8, :]
                        for a in range(2):
                            key = (a, s, c, q)
                            acc[key] = w[a][q] * d + acc[key] if key in acc else w[a][q] * d
        for a in range(2):
            rows = pl.ds(pl.multiple_of(16 * p + 8 * a, 8), 8)
            for s in range(2):
                for ri in range(2):
                    red = []
                    for c in range(2):
                        t1, t2, t3 = (acc[a, s, c, q] for q in range(3))
                        value = t1 + t2 if ri == 0 else t3 - t1 + t2
                        red.append(value + ln.swap(value, 3))
                    q0, q1 = red
                    q0s, q1s = ln.swap(q0, 1), ln.swap(q1, 1)
                    f = jnp.where(ln.low, jnp.where(ln.even, q0, q0s), jnp.where(ln.even, q1s, q1))
                    h = jnp.where(ln.low, jnp.where(ln.even, q1s, q1), jnp.where(ln.even, q0, q0s))
                    x_ref[t, rows, 256 * s + 128 * ri : 256 * s + 128 * ri + 128] = 0.5 * (f + ln.sign * h)
        return 0

    lax.fori_loop(0, groups // 2, pair, 0)


def outer_expand(ln, outs, load, put):
    def one(p, _):
        for s in range(2):
            both = [both_outputs(ln.to_entries(load(p, s, ri)), ln) for ri in range(2)]
            for a in range(2):
                parts = [(both[ri][a], ln.swap(both[ri][a], 2)) for ri in range(2)]
                for r in range(2):
                    put(s, r, 0, 2 * p + a, parts[0][r])
                    put(s, r, 1, 2 * p + a, parts[1][r])
                    put(s, r, 2, 2 * p + a, parts[0][r] + parts[1][r])
        return 0

    lax.fori_loop(0, outs // 2, one, 0)


def outer_sums(devices, outs, groups, load_x, load_d, first, store, unroll):
    ob, kb = outs // 2, groups // 2

    def block(q, r, o0, k0):
        total = {}
        if first is not None:
            total = {(a, k): first(r, q, o0 + a, k0 + 8 * k) for a in range(ob) for k in range(kb)}
        for n in range(devices):
            for s in range(2):
                d = [load_d(n, s, r, q, o0 + a) for a in range(ob)]
                for k in range(kb):
                    x = load_x(n, s, q, k0 + 8 * k)
                    for a in range(ob):
                        total[a, k] = total[a, k] + d[a] * x if (a, k) in total else d[a] * x
        for (a, k), value in total.items():
            store(r, q, o0 + a, k0 + 8 * k, value)

    for q in range(3):
        if unroll:
            for r in range(2):
                for o0 in (0, ob):
                    for k0 in (0, 8 * kb):
                        block(q, r, o0, k0)
            continue

        def one(b, _):
            block(q, lax.rem(b, 2), lax.rem(lax.div(b, 2), 2) * ob, lax.div(b, 4) * (8 * kb))
            return 0

        lax.fori_loop(0, 8, one, 0)


def eight(row):
    return pl.ds(row if isinstance(row, int) else pl.multiple_of(row, 8), 8)


def outer_row(outs, rows, r, q, o, k):
    return ((r * 3 + q) * outs + o) * rows + k


def fold_point(pg, spread, rows, point, bias, scale):
    total = pg[0]
    for n in range(1, pg.shape[0]):
        total = total + pg[n]
    total = total * scale
    outs = total.shape[0] // 4
    for k in range(3):
        rows[k] = total[:, 128 * k : 128 * k + 128]
    blades = [None] * 4
    ones = jnp.ones((8, 128), jnp.bfloat16)
    for a in range(4):
        some = pl.ds(a, outs, stride=4)
        high, low = split(jnp.concatenate([rows[0, some, :], rows[1, some, :]], axis=1))
        for b in range(4):
            dot = functools.partial(lax.dot_general, dimension_numbers=NT, preferred_element_type=jnp.float32)
            value = dot(high, spread[b]) + dot(low, spread[b])
            value = -value if minus_sign(a, b) else value
            blades[a ^ b] = value if blades[a ^ b] is None else blades[a ^ b] + value
        high, low = split(rows[2, some, :])
        bias[a : a + 1, :] = (dot(ones, high) + dot(ones, low))[0:1, :]
    for c in range(4):
        point[:, c, :] = blades[c][:, : point.shape[2]]


def minus_sign(a, b):
    return b == (3 if a < 2 else 1)


def tail_kernel(scale, point_scale, steps, partial, x_ref, d_ref, pg, spread, *refs):
    part_ref, refs = (refs[0], refs[1:]) if partial else (None, refs)
    results, (g_ref, point, bias, *outs_ref), refs = refs[:4], refs[4:11], refs[11:]
    (acc, xd, de, rows3, sems), held = refs[:5], refs[5:]
    ln = Lanes()
    tile, side, step = pl.program_id(0), pl.program_id(1), pl.program_id(2)
    devices, rows = x_ref.shape[0], x_ref.shape[2]
    groups = rows // 8
    outs = d_ref.shape[2] // 4

    def load(i):
        return pltpu.make_async_copy(results[i], held[i], sems.at[0, i])

    def store(i):
        return pltpu.make_async_copy(held[i], outs_ref[i], sems.at[1, i])

    @pl.when((tile == 0) & (side == 0) & (step == 0))
    def _():
        for i in range(4):
            load(i).start()
        fold_point(pg, spread, rows3, point, bias, point_scale)

    @pl.when((tile == 1) & (side == 0) & (step == 0))
    def _():
        for i in range(4):
            load(i).wait()
            store(i).start()

    @pl.when((tile == TILES - 1) & (side == 1) & (step == steps - 1))
    def _():
        for i in range(4):
            store(i).wait()

    @pl.when((side == 0) | (steps > 1))
    def _():
        def expand(n, _):
            def put(s, r, q, o, value):
                de[n, s, r, q, o] = value

            outer_expand(
                ln, outs, lambda p, s, ri: d_ref[n, 0, eight(8 * p), 256 * s + 128 * ri : 256 * s + 128 * ri + 128], put
            )
            return 0

        lax.fori_loop(0, devices, expand, 0)

    def differ(n, _):
        for s in range(2):
            xd[n, s] = x_ref[n, 0, :, 256 * s : 256 * s + 128] - x_ref[n, 0, :, 256 * s + 128 : 256 * s + 256]
        return 0

    lax.fori_loop(0, devices, differ, 0)

    def load_x(n, s, q, row):
        if q == 2:
            return xd[n, s, eight(row), :]
        return x_ref[n, 0, eight(row), 256 * s + 128 * q : 256 * s + 128 * q + 128]

    def first(r, q, o, row):
        if partial:
            return part_ref[0, 0, eight(outer_row(outs, rows, r, q, o, row)), :]
        return jnp.where(step == 0, 0.0, acc[r, q, o, eight(row), :])

    def keep(r, q, o, row, value):
        acc[r, q, o, eight(row), :] = value

    outer_sums(
        devices,
        outs,
        groups,
        load_x,
        lambda n, s, r, q, o: de[n, s, r, q, o],
        first if partial or steps > 1 else None,
        keep,
        True,
    )

    @pl.when(step == steps - 1)
    def _():
        def finish(o, _):
            for g in range(groups):
                where = slice(8 * g, 8 * g + 8)
                for ri in range(2):
                    v = []
                    for r in range(2):
                        t1, t2 = acc[r, 0, o, where, :], acc[r, 1, o, where, :]
                        v.append(t1 + t2 if ri == 0 else acc[r, 2, o, where, :] - t1 + t2)
                    folded = jnp.where(ln.low, v[0], v[1]) + ln.swap(jnp.where(ln.low, v[1], v[0]), 3)
                    out = (folded * ln.sign + ln.swap(folded, 1)) * (0.5 * scale)
                    g_ref[ri, o, 2 * g : 2 * g + 2, :, :] = out.reshape(2, 4, 128)
            return 0

        lax.fori_loop(0, outs, finish, 0)


def tail_pass(x, d, pg, part, results, scale, point_scale):
    count, rows = x.shape[0], x.shape[2]
    own = d.shape[2]
    outs = own // 4
    group = count if count <= 8 else 8
    steps = count // group
    any_space = pl.BlockSpec(memory_space=pl.ANY)
    parts = [] if part is None else [part]
    return pl.pallas_call(
        functools.partial(tail_kernel, scale, point_scale, steps, part is not None),
        grid=(TILES, 2, steps),
        in_specs=[
            pl.BlockSpec((group, 1, rows // 2, 512), lambda t, h, n: (n, t, h, 0)),
            pl.BlockSpec((group, 1, own, 512), lambda t, h, n: (n, t, 0, 0)),
            pl.BlockSpec(pg.shape, lambda t, h, n: (0, 0, 0)),
            pl.BlockSpec((4, 128, 256), lambda t, h, n: (0, 0, 0)),
        ]
        + [pl.BlockSpec((1, 1, *p.shape[2:]), lambda t, h, n: (t, h, 0, 0)) for p in parts]
        + [any_space] * 4,
        out_specs=[
            pl.BlockSpec((2, outs, rows // 8, 4, 128), lambda t, h, n: (0, 0, h, 0, t)),
            pl.BlockSpec((outs, 4, rows // 4), lambda t, h, n: (0, 0, 0)),
            pl.BlockSpec((4, outs), lambda t, h, n: (0, 0)),
        ]
        + [any_space] * 4,
        out_shape=[
            jax.ShapeDtypeStruct((2, outs, rows // 4, 4, MODES), jnp.float32),
            jax.ShapeDtypeStruct((outs, 4, rows // 4), jnp.float32),
            jax.ShapeDtypeStruct((4, outs), jnp.float32),
        ]
        + [jax.ShapeDtypeStruct(r.shape, r.dtype) for r in results],
        scratch_shapes=[
            pltpu.VMEM((2, 3, outs, rows // 2, 128), jnp.float32),
            pltpu.VMEM((group, 2, rows // 2, 128), jnp.float32),
            pltpu.VMEM((group, 2, 2, 3, outs, 8, 128), jnp.float32),
            pltpu.VMEM((3, own, 128), jnp.float32),
            pltpu.SemaphoreType.DMA((2, 4)),
        ]
        + [pltpu.VMEM(r.shape, r.dtype) for r in results],
        compiler_params=pltpu.CompilerParams(vmem_limit_bytes=VMEM_LIMIT),
        cost_estimate=pl.CostEstimate(flops=600 << 20, bytes_accessed=46 << 20, transcendentals=0),
        name="tail_pass",
    )(x, d, pg, jnp.asarray(interleave(rows // 4)), *parts, *results)


MESH = pl.DeviceIdType.MESH


ERFC_SCALE = 0.282842712474619
ERFC = (
    0.11596259978194932,
    0.08090248108382336,
    0.23415924605220384,
    -0.1854802317493698,
    0.3545891457413051,
    -0.10013325473465298,
)


def normal_cdf(u):
    bell = jnp.exp(u * u * -0.5)
    t = 1.0 / (1.0 + ERFC_SCALE * jnp.abs(u))
    tail = ERFC[-1]
    for factor in ERFC[-2::-1]:
        tail = tail * t + factor
    tail = tail * t * bell
    return jnp.where(u >= 0.0, 1.0 - tail, tail), bell


def smem():
    return pl.BlockSpec(memory_space=pltpu.SMEM)


def vmem():
    return pl.BlockSpec(memory_space=pltpu.VMEM)


def grids():
    return ((LB, CB // 4, 0, NB), (LS, CS // 4, NB, NS))


def pieces():
    return [(s, j) for s, (_, count, _, _) in enumerate(grids()) for j in range(count)]


class Place:
    def __init__(self, count):
        self.me = lax.axis_index("chan")
        self.x = self.me // 2
        self.core = self.me % 2
        other, across = 1 - self.core, 1 - self.x
        self.peer = (2 * self.x + other, 2 * across + self.core, 2 * across + other)
        self.other_core, self.other_x = other, across
        self.count = count
        self.dp = lax.axis_index("dp")
        odd, pair = self.dp % 2, self.dp // 2
        self.pos = (1 - odd) * pair + odd * (count - 1 - pair)

    def at_pos(self, p):
        n = self.count
        p = (p + n) % n
        back = p // (n // 2)
        return (1 - back) * (2 * p) + back * (2 * (n - 1 - p) + 1)

    def copy(self, src, dst, send, recv, r):
        return pltpu.make_async_remote_copy(
            src_ref=src,
            dst_ref=dst,
            send_sem=send,
            recv_sem=recv,
            device_id={"chan": self.peer[r]},
            device_id_type=MESH,
        )

    def barrier(self):
        sem = pltpu.get_barrier_semaphore()
        for r in range(3):
            pl.semaphore_signal(sem, inc=1, device_id={"chan": self.peer[r]}, device_id_type=MESH)
        ring = ring_fits(self.count)
        for d in (1, -1) if ring else ():
            pl.semaphore_signal(sem, inc=1, device_id={"dp": self.at_pos(self.pos + d)}, device_id_type=MESH)
        pl.semaphore_wait(sem, 5 if ring else 3)


class ToCells:
    def __init__(self, here, big, small, dst, send, recv, local):
        self.here, self.srcs, self.dst, self.send, self.recv, self.local = here, (big, small), dst, send, recv, local

    def parts(self, s, j, who):
        width, count, first, cells = grids()[s]
        src = self.srcs[s].at[0, :, :, pl.ds(pl.multiple_of(cells * who + width * j, 128), width)]
        return src, self.dst.at[pl.ds(12 * self.here.me, 12), :, pl.ds(first + width * j, width)], s * grids()[0][1] + j

    def to(self, s, j, r):
        src, dst, k = self.parts(s, j, self.here.peer[r])
        return self.here.copy(src, dst, self.send.at[r, k], self.recv.at[r, k], r)

    def own(self, s, j):
        src, dst, k = self.parts(s, j, self.here.me)
        return pltpu.make_async_copy(src, dst, self.local.at[k])

    def across(self, s, j):
        for r in (1, 2):
            self.to(s, j, r).start()

    def near(self, s, j):
        self.to(s, j, 0).start()
        self.own(s, j).start()

    def arrived(self, s, j):
        self.own(s, j).wait()
        for r in range(3):
            self.to(s, j, r).wait_recv()

    def sent(self, s, j):
        for r in range(3):
            self.to(s, j, r).wait_send()


class ToChannels:
    def __init__(self, here, src, big, small, send, recv, local):
        self.here, self.src, self.dsts, self.send, self.recv, self.local = here, src, (big, small), send, recv, local

    def parts(self, s, j, who):
        width, count, first, cells = grids()[s]
        src = self.src.at[pl.ds(12 * who, 12), :, pl.ds(first + width * j, width)]
        lanes = pl.ds(pl.multiple_of(cells * self.here.me + width * j, 128), width)
        return src, self.dsts[s].at[0, :, :, lanes], s * grids()[0][1] + j

    def to(self, s, j, r):
        src, dst, k = self.parts(s, j, self.here.peer[r])
        return self.here.copy(src, dst, self.send.at[r, k], self.recv.at[r, k], r)

    def own(self, s, j):
        src, dst, k = self.parts(s, j, self.here.me)
        return pltpu.make_async_copy(src, dst, self.local.at[k])

    def start(self, s, j):
        for r in (1, 2, 0):
            self.to(s, j, r).start()
        self.own(s, j).start()


class Gather:
    def __init__(self, here, ref, send, recv, own):
        self.here, self.ref, self.send, self.recv, self.own = here, ref, send, recv, own

    def rows(self, t, who):
        return self.ref.at[t, pl.ds(pl.multiple_of(self.own * who, 8), self.own), :]

    def direct(self, t, r):
        block = self.rows(t, self.here.me)
        return self.here.copy(block, block, self.send.at[r, t], self.recv.at[r, t], r)

    def onward(self, t):
        block = self.rows(t, self.here.peer[1])
        return self.here.copy(block, block, self.send.at[2, t], self.recv.at[2, t], 0)

    def start(self, t):
        self.direct(t, 1).start()
        self.direct(t, 0).start()

    def forward(self, t):
        self.direct(t, 1).wait_recv()
        self.onward(t).start()

    def arrived(self, t):
        self.direct(t, 0).wait_recv()
        self.onward(t).wait_recv()

    def sent(self, t):
        self.direct(t, 0).wait_send()
        self.direct(t, 1).wait_send()
        self.onward(t).wait_send()


class SumAll:
    def __init__(self, here, part, first, second, total, send, recv, ln):
        self.here, self.part, self.first, self.second, self.total = here, part, first, second, total
        self.send, self.recv, self.ln = send, recv, ln
        self.half = part.shape[1] // 2

    def rows(self, core):
        return pl.ds(pl.multiple_of(self.half * core, 8), self.half)

    def step(self, k, s, t):
        lanes = pl.ds(256 * s, 256)
        sems = self.send.at[k, s, t], self.recv.at[k, s, t]
        if k == 0:
            src, dst = self.part.at[t, self.rows(self.here.other_core), lanes], self.first.at[t, :, lanes]
            return self.here.copy(src, dst, *sems, 0)
        if k == 1:
            return self.here.copy(self.first.at[t, :, lanes], self.second.at[t, :, lanes], *sems, 1)
        block = self.total.at[t, self.rows(self.here.core), lanes]
        return self.here.copy(block, block, *sems, 0)

    def across(self, s, t):
        self.step(0, s, t).wait()
        lanes = slice(256 * s, 256 * s + 256)
        self.first[t, :, lanes] = self.first[t, :, lanes] + self.part[t, self.rows(self.here.core), lanes]
        self.step(1, s, t).start()

    def back(self, s, t):
        self.step(1, s, t).wait_recv()
        ln = self.ln

        def group(g, _):
            rows = pl.ds(pl.multiple_of(8 * g, 8), 8)
            mine = pl.ds(pl.multiple_of(self.half * self.here.core + 8 * g, 8), 8)
            for ri in range(2):
                lanes = slice(256 * s + 128 * ri, 256 * s + 128 * ri + 128)
                self.total[t, mine, lanes] = ln.to_entries(self.first[t, rows, lanes] + self.second[t, rows, lanes])
            return 0

        lax.fori_loop(0, self.half // 8, group, 0)
        self.step(2, s, t).start()


class SumScatter:
    def __init__(self, here, part, first, second, result, send, recv, lead, width):
        self.here, self.part, self.first, self.second, self.result = here, part, first, second, result
        self.send, self.recv, self.lead, self.width = send, recv, lead, width
        self.own = result.shape[-2]

    def rows(self, ref, t, s, block):
        where = (pl.ds(pl.multiple_of(self.own * block, 8), self.own), pl.ds(self.width * s, self.width))
        return ref.at[(t, *where)] if self.lead else ref.at[where]

    def over(self, s, t, x):
        src = self.rows(self.part, t, s, 2 * x + self.here.other_core)
        return self.here.copy(src, self.rows(self.first, t, s, x), self.send.at[x, s, t], self.recv.at[x, s, t], 0)

    def across_copy(self, s, t):
        src, dst = self.rows(self.first, t, s, self.here.other_x), self.rows(self.second, t, s, 0)
        return self.here.copy(src, dst, self.send.at[2, s, t], self.recv.at[2, s, t], 1)

    def start(self, s, t):
        for x in range(2):
            self.over(s, t, x).start()

    def across(self, s, t):
        for x in range(2):
            self.over(s, t, x).wait_recv()
            slot = self.rows(self.first, t, s, x)
            slot[...] = slot[...] + self.rows(self.part, t, s, 2 * x + self.here.core)[...]
        self.across_copy(s, t).start()

    def finish(self, s, t):
        self.across_copy(s, t).wait_recv()
        result = self.rows(self.result, t, s, 0)
        result[...] = self.rows(self.first, t, s, self.here.x)[...] + self.rows(self.second, t, s, 0)[...]

    def sent(self, s, t):
        for x in range(2):
            self.over(s, t, x).wait_send()
        self.across_copy(s, t).wait_send()


class Ring:
    def __init__(self, here, streams, send, recv):
        self.here, self.streams, self.send, self.recv = here, streams, send, recv
        self.steps = here.count // 2 if ring_fits(here.count) else 0

    def origin(self, way, step):
        return self.here.at_pos(self.here.pos - (step + 1) * (1 - 2 * way))

    def part(self, way, step):
        return way if step == self.steps - 1 else None

    def copies(self, way, step):
        target = self.here.at_pos(self.here.pos + (1 - 2 * way))
        part = self.part(way, step)
        out = []
        for k, place in self.streams:
            out.append(
                pltpu.make_async_remote_copy(
                    src_ref=place(way, step - 1, part),
                    dst_ref=place(way, step, part),
                    send_sem=self.send.at[k, way, step],
                    recv_sem=self.recv.at[k, way, step],
                    device_id={"dp": target},
                    device_id_type=MESH,
                )
            )
        return out

    def start(self, step):
        for way in range(2):
            for cp in self.copies(way, step) if step < self.steps else ():
                cp.start()

    def advance(self, step, then):
        for way in range(2) if step <= self.steps else ():
            for cp in self.copies(way, step - 1):
                cp.wait_recv()
            for cp in self.copies(way, step) if step < self.steps else ():
                cp.start()
            for cp in then(way, step - 1):
                cp.start()

    def first_sent(self):
        for way in range(2) if self.steps else ():
            for cp in self.copies(way, 0):
                cp.wait_send()

    def finish(self, then, first=0, kept=0):
        for way in range(2):
            for step in range(self.steps):
                for cp in self.copies(way, step) if step >= first else ():
                    cp.wait_send()
                for cp in then(way, step) if step >= kept else ():
                    cp.wait()


def ring_fits(count):
    return count == 8


def spectral_piece(z_ref, zh, zl, yh, yl, pre, inverse, phase, chunk, count, s, rows, width):
    vth, vtl, wth, wtl = inverse
    for j in range(count):
        turn_modes(z_ref, zh, zl, phase, chunk + j, s, rows, rows * j)
    used = slice(0, count * rows)
    first_stage(zh[used, :], zl[used, :], vth, vtl, yh, yl, used)

    def tile(n, _):
        lanes = pl.ds(pl.multiple_of(256 * n, 256), 256)
        pre[used, lanes] = dot3(yh[used, :], yl[used, :], wth[:, lanes], wtl[:, lanes])
        return 0

    lax.fori_loop(0, width // 256, tile, 0)


def main_kernel(
    dp_count, live_big, live_small, bias_in, weights, spread, big, small, w, cbig, csmall, tables_in, phases,
    big_out, small_out, big_grad, small_grad, pg_all, gathered,
    tabs, vbuf, cbuf, ob, osm, gb, gs, kh, kl, sh, sl, x1, z1, x2, x2a, x2b, x2t, dza, dzb, dzo, dxo, xs, pgs,
    wm, xe, de, hid, zh, zl, yh, yl, pre, blades, c_own, c_all, square, ch, cl, dh, dl, pg, pga, pgb, pgo,
    load_sem, own_sem, half_sem, chalf_sem, w_sem, local_sem, out_sem, ctd_half_sem,
    v_send, v_recv, c_send, c_recv, o_send, o_recv, d_send, d_recv, p_send, p_recv,
    x1_send, x1_recv, z1_send, z1_recv, z2_send, z2_recv, x2_send, x2_recv,
    dz_send, dz_recv, dx_send, dx_recv, pg_send, pg_recv,
    xr_send, xr_recv, xc_send, xc_recv, dr_send, dr_recv, keep_sem, ready, near_sem, sums_sem,
):
    here = Place(dp_count)
    ln = Lanes()
    pbi, psi, pbo, pso = phases
    rows = x1.shape[1]
    own = rows // 4
    outs = own // 4
    groups = rows // 8
    forward = (tabs[0:4], tabs[4:8])
    inverse = (tabs[8:12], tabs[12:16])
    phase_in, phase_out = (pbi, psi), (pbo, pso)
    own_rows = pl.ds(pl.multiple_of(own * here.me, 8), own)
    loads = [pltpu.make_async_copy(src, dst, load_sem.at[i]) for i, (src, dst) in enumerate(zip(tables_in, tabs))]
    g_planes = [pltpu.make_async_copy(cbig, gb, own_sem.at[2]), pltpu.make_async_copy(csmall, gs, own_sem.at[3])]
    planes = [pltpu.make_async_copy(big, ob, own_sem.at[0]), pltpu.make_async_copy(small, osm, own_sem.at[1])]

    def w_copy(t):
        dst = wm.at[t].reshape(2, outs, rows // 4, 4, 128)
        return pltpu.make_async_copy(w.at[:, :, :, :, pl.ds(128 * t, 128)], dst, w_sem.at[t])

    def point_copy(r):
        return here.copy(c_own, c_all.at[own_rows, :], p_send.at[r], p_recv.at[r], r)

    live = (live_big[0].astype(jnp.float32), live_small[0].astype(jnp.float32))

    fields = ToCells(here, ob, osm, vbuf, v_send, v_recv, half_sem)
    grads = ToCells(here, gb, gs, cbuf, c_send, c_recv, chalf_sem)
    outputs = ToChannels(here, vbuf, big_out, small_out, o_send, o_recv, out_sem)
    backs = ToChannels(here, cbuf, ob, osm, d_send, d_recv, ctd_half_sem)
    x1_gather = Gather(here, x1, x1_send, x1_recv, own)
    z1_gather = Gather(here, z1, z1_send, z1_recv, own)
    z2 = x2
    z2_gather = Gather(here, z2, z2_send, z2_recv, own)
    x2_sum = SumAll(here, x2, x2a, x2b, x2t, x2_send, x2_recv, ln)
    dz_sum = SumScatter(here, x1, dza, dzb, dzo, dz_send, dz_recv, True, 256)
    dx_sum = SumScatter(here, z1, x2a, x2b, dxo, dx_send, dx_recv, True, 512)
    pg_sum = SumScatter(here, pg, pga, pgb, pgo, pg_send, pg_recv, False, PG)
    half_rows = pl.ds(pl.multiple_of(2 * own * here.core, 8), 2 * own)
    lanes_of = (pl.ds(0, 256), pl.ds(256, 256))

    last = dp_count // 2 - 1
    ring = ring_fits(dp_count)
    x2_near, x2_far, dz_far, sums_out = gathered if ring else (None,) * 4

    def far(way, k):
        return 2 if k == last else way

    def span(first, size, part):
        if part is None:
            return pl.ds(first, size)
        return pl.ds(first + part * (size // 2), size // 2)

    def half_span(part):
        size = 2 * own if part is None else own
        first = 2 * own * here.core + (0 if part is None else own * part)
        return pl.ds(pl.multiple_of(first, 8), size)

    def x2_place(s):
        def place(way, k, part):
            if k < 0:
                return x2t.at[:, half_span(part), lanes_of[s]]
            slot = k if k == last else 4 * way + k
            return xs.at[slot, :, span(0, 2 * own, part), lanes_of[s]]

        return place

    def dz_place(s):
        def place(way, k, part):
            if k < 0:
                return dzo.at[:, span(0, own, part), lanes_of[s]]
            ref = x2t if way == 0 or k == last else z2
            return ref.at[:, span(own * k, own, part), lanes_of[s]]

        return place

    def pg_place(way, k, part):
        if k < 0:
            return pgo.at[span(0, own, part), :]
        return pgs.at[k if k == last else 4 * way + k, span(0, own, part), :]

    x2_rings = [Ring(here, [(s, x2_place(s))], xr_send, xr_recv) for s in range(2)]
    dz_rings = [
        Ring(here, [(0, dz_place(0))], dr_send, dr_recv),
        Ring(here, [(1, dz_place(1)), (2, pg_place)], dr_send, dr_recv),
    ]

    def keep_x2(s):
        def keep(way, k):
            part = x2_rings[s].part(way, k)
            slot = x2_place(s)(way, k, part)
            ref = x2_near.at[1 + 2 * k + way] if k < 2 else x2_far.at[far(way, k)]
            block = ref.at[:, half_span(part), lanes_of[s]]
            return (
                here.copy(slot, block, xc_send.at[s, way, k], xc_recv.at[s, way, k], 0),
                pltpu.make_async_copy(slot, block, keep_sem.at[s, way, k]),
            )

        return keep

    def keep_dz(s):
        def keep(way, k):
            ring = dz_rings[s]
            i, part = ring.origin(way, k), ring.part(way, k)
            out = []
            if k > 1:
                block = dz_far.at[far(way, k), :, span(0, own, part), lanes_of[s]]
                out.append(pltpu.make_async_copy(dz_place(s)(way, k, part), block, keep_sem.at[2 + s, way, k]))
            if s == 1:
                block = pg_all.at[i, span(0, own, part), :]
                out.append(pltpu.make_async_copy(pg_place(way, k, part), block, keep_sem.at[4, way, k]))
            return out

        return keep

    def x2_done():
        for s in range(2):
            for way in range(2):
                for k in range(2):
                    for cp in keep_x2(s)(way, k):
                        cp.wait()

    def x2_advance(s, step):
        x2_rings[s].advance(step, keep_x2(s))

    def dz_advance(s, step):
        dz_rings[s].advance(step, keep_dz(s))

    def tell_ready(s):
        if ring_fits(dp_count):
            x2_rings[s].first_sent()
            for way in range(2):
                target = here.at_pos(here.pos + (1 - 2 * way))
                pl.semaphore_signal(ready.at[s], inc=1, device_id={"dp": target}, device_id_type=MESH)

    def dz_start(s):
        if ring_fits(dp_count):
            pl.semaphore_wait(ready.at[s], 2)
            dz_rings[s].start(0)

    for cp in planes + loads[:8]:
        cp.start()
    here.barrier()
    for cp in planes:
        cp.wait()
    for j in range(CS // 4):
        fields.across(1, j)
    for s, j in pieces():
        fields.near(s, j)
    for t in range(TILES):
        w_copy(t).start()
    for cp in loads[8:] + g_planes:
        cp.start()
    for cp in loads[:8]:
        cp.wait()

    for ref, h, l, count, width in ((ob, kh, kl, CB, LB), (osm, sh, sl, CS, LS)):

        def stack(c, _):
            high, low = split(ref[0, :, :, pl.ds(pl.multiple_of(width * c, 128), width)].reshape(own, width))
            where = pl.ds(pl.multiple_of(own * c, 16), own)
            h[where, :] = high
            l[where, :] = low
            return 0

        lax.fori_loop(0, count, stack, 0)

    def own_modes(s):
        h, l, phase, count = ((kh, kl, pbi, CB), (sh, sl, psi, CS))[s]
        wh, wl, vh, vl = forward[s]
        first_stage(h[...], l[...], wh, wl, yh, yl, slice(0, count * own))

        def own_tile(t, _):
            re, im = forward_tile(yh, yl, vh, vl, phase, 0, count, own, t)
            x1[t, own_rows, 256 * s : 256 * s + 128] = re
            x1[t, own_rows, 256 * s + 128 : 256 * s + 256] = im
            if s == 0:
                x1_gather.start(t)
            return 0

        lax.fori_loop(0, TILES, own_tile, 0)

    own_modes(1)
    own_modes(0)
    fields.across(0, 0)
    blades[...] = jnp.zeros_like(blades)
    blades[0, :, : rows // 4] = weights[...].reshape(own, rows // 4)
    dense = jnp.zeros((own, 256), jnp.float32)
    for b in range(4):
        for g in range(own // 8):
            value = blades[0, 8 * g : 8 * g + 8, :]
            value = ln.swap(value, b) if b else value
            minus = (ln.s4 < 2) if b == 3 else (ln.s4 >= 2) if b == 1 else None
            blades[1, 8 * g : 8 * g + 8, :] = value if minus is None else jnp.where(minus, -value, value)
        high, low = split(blades[1])
        dense += jnp.dot(high, spread[b], preferred_element_type=jnp.float32)
        dense += jnp.dot(low, spread[b], preferred_element_type=jnp.float32)
    c_own[:, :256] = dense
    row = lax.broadcasted_iota(jnp.int32, (own, PG - 256), 0)
    column = jnp.zeros((own, PG - 256), jnp.float32)
    for o in range(outs):
        for a in range(4):
            column = jnp.where(row == 4 * o + a, bias_in[a, o], column)
    c_own[:, 256:] = column
    c_all[own_rows, :] = c_own[...]
    for r in range(3):
        point_copy(r).start()

    for t in range(TILES):
        w_copy(t).wait()

        def convert(i, _):
            ri, o = lax.rem(i, 2), lax.div(i, 2)
            for g in range(groups):
                where = slice(8 * g, 8 * g + 8)
                wm[t, ri, o, where, :] = ln.to_matrix(wm[t, ri, o, where, :])
            return 0

        lax.fori_loop(0, 2 * outs, convert, 0)
        x1_gather.forward(t)

    def mix_first(t, _):
        x1_gather.arrived(t)
        mix_tile(wm, t, lambda where, lanes: ln.to_entries(x1[t, where, lanes]), z1, here.me, xe, ln)
        z1_gather.start(t)

        @pl.when(t >= 1)
        def _():
            z1_gather.forward(t - 1)

        return 0

    lax.fori_loop(0, TILES, mix_first, 0)
    for cp in g_planes:
        cp.wait()
    z1_gather.forward(TILES - 1)
    fields.across(0, 1)
    fields.across(0, 2)
    grads.across(0, 0)
    for s, j in pieces():
        grads.near(s, j)
    for r in range(3):
        point_copy(r).wait_recv()
    square[0:rows, :] = c_all[:, :256]
    square[rows:256, :] = jnp.zeros((256 - rows, 256), jnp.float32)
    ch[...], cl[...] = split(c_all[:, :rows])
    dh[...], dl[...] = split(jnp.transpose(square[...])[:rows, :rows])

    for cp in loads[8:]:
        cp.wait()

    def pointwise(s, j, load, store):
        width, count, first, cells_here = grids()[s]

        def cells(n, _):
            lanes = pl.ds(pl.multiple_of(first + j * width + 256 * n, 256), 256)
            vh, vl = split(load(lanes))
            store(lanes, dot3(ch[...], cl[...], vh, vl) + c_all[:, 256:257])
            return 0

        lax.fori_loop(0, width // 256, cells, 0)

    def load_field(lanes):
        return vbuf[:, :, lanes].reshape(rows, 256)

    def store_field(lanes, value):
        vbuf[:, :, lanes] = value.reshape(rows // 4, 4, 256)

    def load_hid(lanes):
        return hid[:, lanes]

    def store_hid(lanes, value):
        hid[:, lanes] = value

    def point_piece(s, j):
        fields.arrived(s, j)
        pointwise(s, j, load_field, store_hid)

    for j in range(CS // 4):
        point_piece(1, j)
    point_piece(0, 0)

    def z1_arrived(t, _):
        z1_gather.arrived(t)
        return 0

    lax.fori_loop(0, TILES, z1_arrived, 0)

    def each_tile(fn):
        def one(t, _):
            fn(t)
            return 0

        lax.fori_loop(0, TILES, one, 0)

    for s, (width, count, first, cells_here) in enumerate(grids()):
        wh, wl, vh, vl = forward[s]
        chunk = here.me * count
        spectral_piece(z1, zh, zl, yh, yl, pre, inverse[s], phase_out[s], chunk, count, s, rows, width)
        if s == 1:
            each_tile(lambda t: x2_sum.across(0, t))
        for j in range(count):
            if s == 0 and j > 0:
                point_piece(0, j)

            def cells(n, _):
                at = pl.ds(pl.multiple_of(256 * n, 256), 256)
                lanes = pl.ds(pl.multiple_of(first + j * width + 256 * n, 256), 256)
                u = pre[rows * j : rows * (j + 1), at] + hid[:, lanes]
                out = load_field(lanes) + u * normal_cdf(u)[0]
                hid[:, lanes] = out
                oh, ol = split(out)
                kh[rows * j : rows * (j + 1), at] = oh
                kl[rows * j : rows * (j + 1), at] = ol
                return 0

            lax.fori_loop(0, width // 256, cells, 0)
        if s == 1:
            each_tile(lambda t: x2_sum.back(0, t))
            x2_rings[0].start(0)

        used = slice(0, count * rows)
        first_stage(kh[used, :width], kl[used, :width], wh, wl, yh, yl, used)

        def modes(t, _):
            re, im = forward_tile(yh, yl, vh, vl, phase_in[s], chunk, count, rows, t)
            x2[t, :, 256 * s : 256 * s + 128] = re
            x2[t, :, 256 * s + 128 : 256 * s + 256] = im
            x2_sum.step(0, s, t).start()
            return 0

        lax.fori_loop(0, TILES, modes, 0)
    for s, j in pieces():
        fields.sent(s, j)
    each_tile(lambda t: x2_sum.across(1, t))
    each_tile(lambda t: x2_sum.back(1, t))
    x2_rings[1].start(0)

    def crossed(t):
        for s in range(2):
            x2_sum.step(1, s, t).wait_send()

    each_tile(crossed)

    def mix_second(t, _):
        for s in range(2):
            x2_sum.step(2, s, t).wait_recv()
        mix_tile(wm, t, lambda where, lanes: x2t[t, where, lanes], z2, here.me, xe, ln)
        z2_gather.start(t)

        @pl.when(t >= 1)
        def _():
            z2_gather.forward(t - 1)

        return 0

    lax.fori_loop(0, TILES // 2, mix_second, 0)
    x2_advance(0, 1)
    lax.fori_loop(TILES // 2, TILES, mix_second, 0)
    x2_local = pltpu.make_async_copy(x2t, x2_near.at[0] if ring else gathered[0], local_sem.at[0])
    x2_local.start()
    z2_gather.forward(TILES - 1)
    grads.across(0, 1)
    grads.across(0, 2)
    for j in range(CS // 4):
        grads.across(1, j)
    for s, j in pieces():
        pointwise(s, j, load_hid, store_field)
    x2_advance(1, 1)
    each_tile(z2_gather.arrived)
    x2_advance(0, 2)
    each_tile(x1_gather.sent)
    each_tile(z1_gather.sent)
    pg[...] = jnp.zeros_like(pg)

    for s, (width, count, first, cells_here) in enumerate(grids()):
        wh, wl, vh, vl = forward[s]
        chunk = here.me * count
        spectral_piece(z2, zh, zl, yh, yl, pre, inverse[s], phase_out[s], chunk, count, s, rows, width)
        if s == 0:
            x2_local.wait()
            each_tile(z2_gather.sent)
        each_tile(lambda t: x2_sum.step(2, s, t).wait_send())
        tell_ready(s)
        if s == 1:
            each_tile(lambda t: dz_sum.across(0, t))
            backs.start(0, 0)
        for j in range(count):
            grads.arrived(s, j)

            def cells(n, _):
                at = pl.ds(pl.multiple_of(256 * n, 256), 256)
                lanes = pl.ds(pl.multiple_of(first + j * width + 256 * n, 256), 256)
                value = hid[:, lanes]
                vh, vl = split(value)
                u = pre[rows * j : rows * (j + 1), at] + load_field(lanes)
                cdf, bell = normal_cdf(u)
                store_field(lanes, value + u * cdf)
                slope = cdf + u * (bell * (1.0 / math.sqrt(2.0 * math.pi)))
                grad = cbuf[:, :, lanes].reshape(rows, 256) * live[s] * slope
                gh, gl = split(grad)
                kh[rows * j : rows * (j + 1), at] = gh
                kl[rows * j : rows * (j + 1), at] = gl
                cbuf[:, :, lanes] = dot3(dh[...], dl[...], gh, gl).reshape(rows // 4, 4, 256)
                pg[:, :rows] += dot3(gh, gl, vh, vl, NT)
                pg[:, 256:] += grad[:, :128] + grad[:, 128:]
                return 0

            lax.fori_loop(0, width // 256, cells, 0)
            if (s, j) == (0, 1):
                x2_advance(1, 2)
        if s == 1:
            each_tile(lambda t: dz_sum.finish(0, t))
            dz_start(0)

        used = slice(0, count * rows)
        first_stage(kh[used, :width], kl[used, :width], wh, wl, yh, yl, used)

        def modes(t, _):
            re, im = forward_tile(yh, yl, vh, vl, phase_out[s], chunk, count, rows, t)
            x1[t, :, 256 * s : 256 * s + 128] = re
            x1[t, :, 256 * s + 128 : 256 * s + 256] = im
            dz_sum.start(s, t)
            return 0

        lax.fori_loop(0, TILES, modes, 0)
        x2_advance(s, 3)
    pg_sum.start(0, 0)
    each_tile(lambda t: dz_sum.across(1, t))
    pg_sum.across(0, 0)
    backs.start(0, 1)
    backs.start(0, 2)
    for j in range(CS // 4):
        backs.start(1, j)
    each_tile(lambda t: dz_sum.finish(1, t))
    pg_sum.finish(0, 0)
    dz_start(1)
    dz_local = [pltpu.make_async_copy(pgo, pg_all.at[here.dp] if ring else pg_all, local_sem.at[2])]
    if not ring:
        dz_local.append(pltpu.make_async_copy(dzo, gathered[1], local_sem.at[1]))
    for cp in dz_local:
        cp.start()

    for t in range(TILES):
        unmix_tile(wm, t, dzo, z1, xe, ln)
        dx_sum.start(0, t)
        if t >= 1:
            dx_sum.across(0, t - 1)
        if t == 1:
            dz_advance(0, 1)
    dx_sum.across(0, TILES - 1)
    for s, j in pieces():
        outputs.start(s, j)
    dz_advance(1, 1)
    dz_advance(0, 2)

    flat = wm.reshape(TILES * 2 * outs * rows, 128)
    half = rows // 2
    acc_rows = 6 * outs * half
    xd_row0 = 2 * acc_rows

    def x_near(i):
        t, h = lax.div(i, 2), lax.rem(i, 2)
        out = []
        for n in range(NEAR):
            src = x2_near.at[n, t, pl.ds(pl.multiple_of(half * h, 8), half), :]
            dst = hid.at[pl.ds(pl.multiple_of(half * h, 8), half), pl.ds(512 * n, 512)]
            out.append(pltpu.make_async_copy(src, dst, near_sem.at[h, n]))
        return out

    def sums_copy(i):
        t, h = lax.div(i, 2), lax.rem(i, 2)
        src = flat.at[pl.ds(pl.multiple_of(acc_rows * h, 8), acc_rows), :]
        return pltpu.make_async_copy(src, sums_out.at[t, h], sums_sem.at[h])

    def de_at(n, s, r, q, o):
        return eight(((((n * 2 + s) * 2 + r) * 3 + q) * outs + o) * 8)

    def near_step(i, _):
        t, h = lax.div(i, 2), lax.rem(i, 2)
        for cp in x_near(i):
            cp.wait()

        @pl.when(i + 1 < 2 * TILES)
        def _():
            for cp in x_near(i + 1):
                cp.start()

        @pl.when(i >= 2)
        def _():
            sums_copy(i - 2).wait()

        @pl.when(h == 0)
        def _():
            for n, (ref, row0) in enumerate(((dzo, 0), (x2t, 0), (z2, 0), (x2t, own), (z2, own))):

                def put(s, r, q, o, value):
                    de[de_at(n, s, r, q, o), :] = value

                outer_expand(
                    ln, outs, lambda p, s, ri: ref[t, eight(row0 + 8 * p), 256 * s + 128 * ri : 256 * s + 128 * ri + 128], put
                )

        def x_row(row):
            return eight(h * half + row)

        def differ(g, _):
            for n in range(NEAR):
                for s in range(2):
                    x = hid[x_row(8 * g), 512 * n + 256 * s : 512 * n + 256 * s + 256]
                    flat[eight(xd_row0 + (n * 2 + s) * half + 8 * g), :] = x[:, :128] - x[:, 128:]
            return 0

        lax.fori_loop(0, half // 8, differ, 0)

        def load_x(n, s, q, row):
            if q == 2:
                return flat[eight(xd_row0 + (n * 2 + s) * half + row), :]
            lane = 512 * n + 256 * s + 128 * q
            return hid[x_row(row), lane : lane + 128]

        def keep_sum(r, q, o, row, value):
            flat[eight(acc_rows * h + outer_row(outs, half, r, q, o, row)), :] = value

        outer_sums(
            NEAR, outs, half // 8, load_x, lambda n, s, r, q, o: de[de_at(n, s, r, q, o), :], None, keep_sum, False
        )
        sums_copy(i).start()
        return 0

    def near_products(lo, hi):
        if ring:
            lax.fori_loop(lo, hi, near_step, 0)

    if ring:
        x2_done()
        for cp in x_near(0):
            cp.start()
        dz_advance(1, 2)
    near_products(0, 2)
    dz_advance(0, 3)
    near_products(2, 4)
    each_tile(lambda t: dx_sum.finish(0, t))
    dz_advance(1, 3)

    for s, (g, o, dst, phase, count, width) in enumerate(
        ((gb, ob, big_grad, pbi, CB, LB), (gs, osm, small_grad, psi, CS, LS))
    ):
        vth, vtl, wth, wtl = inverse[s]
        for j in range(count):
            turn_modes(dxo, zh, zl, phase, j, s, own, own * j)
        for j in range(count // 4):
            backs.own(s, j).wait()
            for r in range(3):
                backs.to(s, j, r).wait_recv()
        used = slice(0, count * own)
        first_stage(zh[used, :], zl[used, :], vth, vtl, yh, yl, used)

        def tile(n, _):
            lanes = pl.ds(pl.multiple_of(256 * n, 256), 256)
            part = dot3(yh[used, :], yl[used, :], wth[:, lanes], wtl[:, lanes])
            for j in range(count):
                where = pl.ds(pl.multiple_of(width * j + 256 * n, 256), 256)
                o[0, :, :, where] = (
                    part[own * j : own * (j + 1)].reshape(outs, 4, 256) + g[0, :, :, where] * live[s] + o[0, :, :, where]
                )
            return 0

        lax.fori_loop(0, width // 256, tile, 0)
        if s == 0:
            near_products(4, 6)
        pltpu.make_async_copy(o, dst, local_sem.at[3 + s]).start()
    near_products(6, 8)
    for s in range(2):
        x2_advance(s, 4)
        dz_advance(s, 4)

    for cp in dz_local:
        cp.wait()
    pltpu.make_async_copy(ob, big_grad, local_sem.at[3]).wait()
    pltpu.make_async_copy(osm, small_grad, local_sem.at[4]).wait()
    for r in range(3):
        point_copy(r).wait_send()
    for s, j in pieces():
        grads.sent(s, j)
        for r in range(3):
            backs.to(s, j, r).wait_send()
        outputs.own(s, j).wait()
        for r in range(3):
            outputs.to(s, j, r).wait()

    def last_tile(t, _):
        for s in range(2):
            dz_sum.sent(s, t)
        dx_sum.sent(0, t)
        return 0

    lax.fori_loop(0, TILES, last_tile, 0)
    pg_sum.sent(0, 0)
    for i in range(2 * TILES - 2, 2 * TILES) if ring else ():
        sums_copy(i).wait()
    for s in range(2):
        x2_rings[s].finish(keep_x2(s), 1, 2)
        dz_rings[s].finish(keep_dz(s))


def main_pass(dp, live_big, live_small, bias, weights, big, small, w, cbig, csmall, tabs):
    rows = w.shape[2] * 4
    outs = w.shape[1]
    own = rows // 4
    any_space = pl.BlockSpec(memory_space=pl.ANY)
    table = tabs["table"]
    phases = (tabs["pb_in"], tabs["ps_in"], tabs["pb_out"], tabs["ps_out"])
    f32, bf16 = jnp.float32, jnp.bfloat16

    def buf(*shape, dtype=f32):
        return pltpu.VMEM(shape, dtype)

    def dma(*shape):
        return pltpu.SemaphoreType.DMA(shape)

    modes = (TILES, rows, 512)
    half, quarter = (TILES, rows // 2, 512), (TILES, own, 512)
    ring = ring_fits(dp)
    steps = max(1, dp // 2) if ring else 1
    slots = 7 if ring else 1
    lead = (dp,) if ring else ()
    if ring:
        shapes = ((NEAR, *modes), (dp - NEAR, *modes), (dp - NEAR, *quarter), (TILES, 2, 3 * outs * rows, 128))
    else:
        shapes = (modes, quarter)
    gathered = tuple(jax.ShapeDtypeStruct(shape, f32) for shape in shapes)
    chunks = (CB + CS) // 4
    return pl.pallas_call(
        functools.partial(main_kernel, dp),
        in_specs=[smem()] * 3 + [vmem()] * 2 + [any_space] * 5 + [(any_space,) * len(table), (vmem(),) * 4],
        out_specs=[any_space] * 5 + [tuple(any_space for _ in gathered)],
        out_shape=[
            jax.ShapeDtypeStruct(big.shape, f32),
            jax.ShapeDtypeStruct(small.shape, f32),
            jax.ShapeDtypeStruct(big.shape, f32),
            jax.ShapeDtypeStruct(small.shape, f32),
            jax.ShapeDtypeStruct((*lead, own, PG), f32),
            gathered,
        ],
        scratch_shapes=[
            tuple(pltpu.VMEM(a.shape, bf16) for a in table),
            buf(rows // 4, 4, NQ),
            buf(rows // 4, 4, NQ),
            buf(*big.shape),
            buf(*small.shape),
            buf(*big.shape),
            buf(*small.shape),
            buf(own * CB, LB, dtype=bf16),
            buf(own * CB, LB, dtype=bf16),
            buf(own * CS, LS, dtype=bf16),
            buf(own * CS, LS, dtype=bf16),
            buf(*modes),
            buf(*modes),
            buf(*modes),
            buf(*half),
            buf(*half),
            buf(*modes),
            buf(*half),
            buf(*quarter),
            buf(*quarter),
            buf(*quarter),
            buf(slots, *half),
            buf(slots, own, PG),
            buf(TILES, 2, outs, rows, 128),
            buf(2, 2, 3, rows, 128),
            buf(NEAR * 12 * outs * 8 if ring else 8, 128),
            buf(rows, NQ),
            buf(own * CB, 2 * MODES, dtype=bf16),
            buf(own * CB, 2 * MODES, dtype=bf16),
            buf(own * CB, 256, dtype=bf16),
            buf(own * CB, 256, dtype=bf16),
            buf(own * CB, LB),
            buf(2, own, 128),
            buf(own, PG),
            buf(rows, PG),
            buf(256, 256),
            buf(rows, rows, dtype=bf16),
            buf(rows, rows, dtype=bf16),
            buf(rows, rows, dtype=bf16),
            buf(rows, rows, dtype=bf16),
            buf(rows, PG),
            buf(2 * own, PG),
            buf(own, PG),
            buf(own, PG),
            dma(len(table)),
            dma(4),
            dma(chunks),
            dma(chunks),
            dma(TILES),
            dma(5),
            dma(chunks),
            dma(chunks),
        ]
        + [dma(3, chunks)] * 8
        + [dma(3)] * 2
        + [dma(3, TILES)] * 6
        + [dma(3, 2, TILES)] * 2
        + [dma(3, 2, TILES)] * 2
        + [dma(3, 1, TILES)] * 2
        + [dma(3, 1, 1)] * 2
        + [dma(2, 2, steps)] * 4
        + [dma(3, 2, steps)] * 2
        + [dma(5, 2, steps), pltpu.SemaphoreType.REGULAR((2,)), dma(2, NEAR), dma(2)],
        compiler_params=pltpu.CompilerParams(vmem_limit_bytes=VMEM_LIMIT, collective_id=0, has_side_effects=True),
        cost_estimate=pl.CostEstimate(flops=40 << 30, bytes_accessed=60 << 20, transcendentals=0),
        name="main_pass",
    )(live_big, live_small, bias, weights, jnp.asarray(interleave(rows // 4)), big, small, w, cbig, csmall, table, phases)


def tables():
    tabs = {}
    forward, inverse = [], []
    for name, side in (("b", HB), ("s", HS)):
        for part in (column_table(side), row_table(side)):
            forward += [jnp.asarray(a) for a in pair_of(part)]
        for part in (row_table(side), column_table(side)):
            inverse += [jnp.asarray(np.ascontiguousarray(a.T)) for a in pair_of(part)]
        tabs[f"p{name}_in"] = jnp.asarray(chunk_phase(side, "in"))
        tabs[f"p{name}_out"] = jnp.asarray(chunk_phase(side, "out"))
    tabs["table"] = tuple(forward + inverse)
    return tabs


def body(
    big_input,
    small_input,
    spectral_weight,
    point_weight,
    point_bias,
    big_cotangent,
    small_cotangent,
    big_live,
    small_live,
):
    dp = lax.axis_size("dp")
    tabs = tables()
    *results, pg_all, gathered = main_pass(
        dp,
        big_live,
        small_live,
        point_bias.T,
        jnp.transpose(point_weight, (0, 2, 1)),
        big_input,
        small_input,
        spectral_weight,
        big_cotangent,
        small_cotangent,
        tabs,
    )
    if ring_fits(dp):
        _, x2_all, dz_all, part = gathered
    else:
        x2_all, dz_all, pg_all = lax.all_gather((*gathered, pg_all), "dp")
        part = None
    samples = 2 * dp
    pixels = (HB * HB + HS * HS) * dp
    spec, point, bias, *results = tail_pass(
        x2_all, dz_all, pg_all, part, results, 1.0 / math.sqrt(samples), 1.0 / math.sqrt(pixels)
    )
    return (*results, spec, jnp.transpose(point, (0, 2, 1)), bias.T)


def solution(mesh):
    in_specs = (
        P("dp", "chan", None, None),
        P("dp", "chan", None, None),
        P(None, "chan", None, None, None),
        P("chan", None, None),
        P("chan", None),
        P("dp", "chan", None, None),
        P("dp", "chan", None, None),
        P("dp"),
        P("dp"),
    )
    out_specs = (
        P("dp", "chan", None, None),
        P("dp", "chan", None, None),
        P("dp", "chan", None, None),
        P("dp", "chan", None, None),
        P(None, "chan", None, None, None),
        P("chan", None, None),
        P("chan", None),
    )
    return jax.shard_map(body, mesh=mesh, in_specs=in_specs, out_specs=out_specs, check_vma=False)
```

time: 1920 us -> 230 us (0.12)
  matrix products: 787 us -> 0 us
  local copies, waits for them, and re-layouts: 384 us -> 0 us
  waiting for transfers between devices: 370 us -> 0 us
  other arithmetic: 315 us -> 0 us
  Pallas kernels: 0 us -> 228 us
  blocking collectives: 37.3 us -> 0 us
    dot_general x80 -> x0, matrix products: 787 us -> none  [the longest x6 127 us: mix_modes(): jnp.einsum('ojk,bjk->bok', dense_real, modes_real, precision=highest)]
    psum x1 -> x0, waiting for transfers between devices: 297 us -> none  [body(): lax.psum((grad_spec, grad_point, grad_bias), 'dp')]
    reshape x26 -> x0, local copies, waits for them, and re-layouts: 246 us -> none  [the longest x9 181 us: clifford_dense(): dense_stack.reshape((dense_shape[0] * 4, dense_shape[2] * 4) + dense_shap...]
    pallas_call x0 -> x2, Pallas kernels: none -> 228 us  [the longest x1 203 us: main_pass(): pl.pallas_call(functools.partial(main_kernel, dp), in_specs=[smem()] * 3...]
    another operation x28 -> x0, local copies, waits for them, and re-layouts: 106 us -> none
    another operation x29 -> x0, other arithmetic: 92.1 us -> none  [the longest x12 46.7 us: clifford_dense(): outer_list.append(jnp.stack(inner_list, axis=2))]
    broadcast_in_dim x4 -> x0, other arithmetic: 76 us -> none  [the longest x2 39.1 us: mix_modes(): dense_real = clifford_dense(kernel[0])]
    mul x20 -> x0, other arithmetic: 68.1 us -> none  [the longest x13 56.1 us: clifford_dense(): blade_sign[out_blade][in_blade]]
  transfers between devices with their start and end apart: 6 -> 0, of which waited for: 3 -> 0; matrix products, arithmetic and copies ran while one was open for 37% -> 0% of each run, Pallas kernels for 0% -> 0%
where the time goes in v1:
time: 230 us
  Pallas kernels  228 us (99%)
    pallas_call x1, Pallas kernels, main_pass(): pl.pallas_call(functools.partial(main_kernel, dp), in_specs=[smem()] * 3...  203 us
    pallas_call x1, Pallas kernels, tail_pass(): pl.pallas_call(functools.partial(tail_kernel, scale, point_scale, steps,...  25.2 us

profile of v1, /device:TPU:0, one launch (start us, length us, event | category | flops | bytes accessed | tf_op | source)
XLA Modules:
  0.0 230.2 jit_solution(120110209055332810)
XLA Ops:
  1.9 202.9 %main_pass.1 = (f32[1,12,4,9216]{3,2,1,0:T(4,128)}, f32[1,12,4,4096]{3,2,1,0:T(4,128)}, f32[1,12,4,9216]{3,2,1,0:T(4,128)}, f32[1,12,4,4096]{3,2,1,0:T(4,128)}, ...) custom-call(s32[1]{0:T(128)S(6)} %copy.38.live_big, ...), custom_call_target="tpu_custom_call" | custom-call | flops 42949672960 | bytes 62914560 | tf_op jit(solution)/shard_map/main_pass/pallas_call | solution.py:1466
  204.8 25.2 %tail_pass.1 = (f32[2,12,48,4,512]{4,3,2,1,0:T(4,128)}, f32[12,4,48]{2,1,0:T(4,128)}, f32[4,12]{1,0:T(4,128)}, f32[1,12,4,9216]{3,2,1,0:T(4,128)}, f32[1,12,4,40...) custom-call(f32[3,4,192,512]{3,2,1,0:T(8,128)} %get-tuple-element.22.x_ref, ...), custom_call_target="tpu_custom_call" | custom-call | flops 629145600 | bytes 48234496 | tf_op jit(solution)/shard_map/tail_pass/pallas_call | solution.py:459

commit v2 on v1

--- a/solution.py
+++ b/solution.py
@@ -1014,7 +1014,6 @@
 
     own_modes(1)
     own_modes(0)
-    fields.across(0, 0)
     blades[...] = jnp.zeros_like(blades)
     blades[0, :, : rows // 4] = weights[...].reshape(own, rows // 4)
     dense = jnp.zeros((own, 256), jnp.float32)
@@ -1066,8 +1065,8 @@
     for cp in g_planes:
         cp.wait()
     z1_gather.forward(TILES - 1)
-    fields.across(0, 1)
-    fields.across(0, 2)
+    for j in range(CB // 4):
+        fields.across(0, j)
     grads.across(0, 0)
     for s, j in pieces():
         grads.near(s, j)
@@ -1110,7 +1109,6 @@
 
     for j in range(CS // 4):
         point_piece(1, j)
-    point_piece(0, 0)
 
     def z1_arrived(t, _):
         z1_gather.arrived(t)
@@ -1132,7 +1130,7 @@
         if s == 1:
             each_tile(lambda t: x2_sum.across(0, t))
         for j in range(count):
-            if s == 0 and j > 0:
+            if s == 0:
                 point_piece(0, j)
 
             def cells(n, _):

time: 230 us -> 231 us (level)
  no operation moved by 1% of the time
where the time goes in v2:
time: 231 us
  Pallas kernels  228 us (99%)
    pallas_call x1, Pallas kernels, main_pass(): pl.pallas_call(functools.partial(main_kernel, dp), in_specs=[smem()] * 3...  203 us
    pallas_call x1, Pallas kernels, tail_pass(): pl.pallas_call(functools.partial(tail_kernel, scale, point_scale, steps,...  25.2 us

profile of v2, /device:TPU:0, one launch (start us, length us, event | category | flops | bytes accessed | tf_op | source)
XLA Modules:
  0.0 230.6 jit_solution(16295262633083561951)
XLA Ops:
  1.9 203.3 %main_pass.1 = (f32[1,12,4,9216]{3,2,1,0:T(4,128)}, f32[1,12,4,4096]{3,2,1,0:T(4,128)}, f32[1,12,4,9216]{3,2,1,0:T(4,128)}, f32[1,12,4,4096]{3,2,1,0:T(4,128)}, ...) custom-call(s32[1]{0:T(128)S(6)} %copy.38.live_big, ...), custom_call_target="tpu_custom_call" | custom-call | flops 42949672960 | bytes 62914560 | tf_op jit(solution)/shard_map/main_pass/pallas_call | solution.py:1464
  205.2 25.2 %tail_pass.1 = (f32[2,12,48,4,512]{4,3,2,1,0:T(4,128)}, f32[12,4,48]{2,1,0:T(4,128)}, f32[4,12]{1,0:T(4,128)}, f32[1,12,4,9216]{3,2,1,0:T(4,128)}, f32[1,12,4,40...) custom-call(f32[3,4,192,512]{3,2,1,0:T(8,128)} %get-tuple-element.22.x_ref, ...), custom_call_target="tpu_custom_call" | custom-call | flops 629145600 | bytes 48234496 | tf_op jit(solution)/shard_map/tail_pass/pallas_call | solution.py:459
